TPU v7x, 512 devices: a whole 4x4x16 slice. The times are simulated.
512 devices in a mesh: inst: 64 (over z, y), tp: 8 (over x, core).
Axes of the slice: x: 4, y: 4, z: 16, core: 2. Of those that a mesh axis runs over, the one named last changes fastest.
Arguments:
- queries: bfloat16 [512, 8192], P(('inst', 'tp')), may hold values from -6 to 6
- kv_pool: bfloat16 [2, 2048, 256, 1024], P(None, 'inst', None, 'tp'), may hold values from -6 to 6
- block_table: int32 [512, 4], P('inst'), may hold values from 0 to 2047, as said below
- lengths: int32 [512], P('inst'), may hold values from 1 to 1024, as said below
Outputs:
- attended: bfloat16 [512, 8192], P(('inst', 'tp'))
Inputs may be any that keep to these rules, and one draw needn't show every extreme that they name: `block_table`: every number from 0 to 2047 appears exactly once; a slot number divided by 32 is the instance whose pool holds the block, its remainder the slot in that pool. `lengths`: some row has exactly 1024 tokens.
All inputs are finite; a program needn't handle non-finite values.
Results may differ from a plain program's by a relative error of at most 0.0041.
Values may be sent and summed in bfloat16 or wider, within the bound.
No kernel may reach another device: no remote copies, remote signals or barrier semaphores. Data moves between devices by JAX's collectives and lax.ppermute only.
A program may use at most 64 MiB of HBM per device.

v0:
```python
import math

import jax
import jax.numpy as jnp
from jax import lax
from jax.sharding import PartitionSpec as P

H = 64
KVH = 8
HD = 128


def per_device(queries, kv_pool, block_table, lengths):
    holder = lax.axis_index("inst")
    local_query = lax.all_to_all(queries, "tp", split_axis=1, concat_axis=0, tiled=True)
    all_queries, all_tables, all_lengths = (
        lax.all_gather(local_query, "inst", axis=0, tiled=True),
        lax.all_gather(block_table, "inst", axis=0, tiled=True),
        lax.all_gather(lengths, "inst", axis=0, tiled=True),
    )
    pool_slots = kv_pool.shape[1]
    block_len = kv_pool.shape[2]
    pool_width = kv_pool.shape[3]
    kv_local = pool_width // HD
    group_size = H // KVH
    heads_here = kv_local * group_size
    max_blocks = block_table.shape[1]
    inst_rows = block_table.shape[0]
    score_scale = 1.0 / math.sqrt(HD)
    flat_ids = all_tables.reshape(-1)
    own_slots = holder * pool_slots + jnp.arange(pool_slots, dtype=jnp.int32)
    matches = flat_ids[None, :] == own_slots[:, None]
    entry_index = jnp.sum(
        jnp.where(matches, jnp.arange(flat_ids.shape[0], dtype=jnp.int32)[None, :], 0), axis=1
    )
    user_row = entry_index // max_blocks
    user_block = entry_index % max_blocks
    filled = jnp.clip(jnp.take(all_lengths, user_row) - user_block * block_len, 0, block_len)
    in_use = filled > 0
    slot_query = jnp.take(all_queries, user_row, axis=0).reshape(
        pool_slots, kv_local, group_size, HD
    )
    slot_keys = kv_pool[0].reshape(pool_slots, block_len, kv_local, HD)
    slot_values = kv_pool[1].reshape(pool_slots, block_len, kv_local, HD)
    scores = (
        jnp.einsum("skgd,stkd->skgt", slot_query, slot_keys, preferred_element_type=jnp.float32)
        * score_scale
    )
    token_mask = (jnp.arange(block_len)[None, :] < filled[:, None])[:, None, None, :]
    scores = jnp.where(token_mask, scores, -1e30)
    block_peak = jnp.max(scores, axis=3)
    exponent = jnp.where(token_mask, jnp.exp(scores - block_peak[..., None]), 0.0)
    block_sum = jnp.sum(exponent, axis=3)
    weights = exponent.astype(jnp.bfloat16)
    mixture = jnp.einsum(
        "skgt,stkd->skgd", weights, slot_values, preferred_element_type=jnp.float32
    )
    partial_value = mixture / jnp.where(in_use[:, None, None], block_sum, 1.0)[..., None]
    partial_value = partial_value.reshape(pool_slots, heads_here * HD)
    block_peak = jnp.where(in_use[:, None], block_peak.reshape(pool_slots, heads_here), -1e30)
    block_sum = jnp.where(in_use[:, None], block_sum.reshape(pool_slots, heads_here), 0.0)
    own_ok = jnp.arange(max_blocks)[None, :] * block_len < lengths[:, None]
    running_max = jnp.full((inst_rows, heads_here), -1e30, jnp.float32)
    numerator = jnp.zeros((inst_rows, heads_here * HD), jnp.float32)
    piece_out = lax.all_gather(partial_value, "inst", axis=0, tiled=True)
    piece_peak = lax.all_gather(block_peak, "inst", axis=0, tiled=True)
    piece_sum = lax.all_gather(block_sum, "inst", axis=0, tiled=True)
    piece_rows = piece_out.shape[0]
    inside = (block_table >= 0) & (block_table < piece_rows) & own_ok
    position = jnp.clip(block_table, 0, piece_rows - 1)
    found_peak = jnp.where(inside[..., None], jnp.take(piece_peak, position, axis=0), -1e30)
    found_sum = jnp.take(piece_sum, position, axis=0)
    found_out = jnp.take(piece_out, position, axis=0).reshape(inst_rows, max_blocks, heads_here, HD)
    new_max = jnp.maximum(running_max, jnp.max(found_peak, axis=1))
    rescale = jnp.exp(running_max - new_max)
    factor = jnp.where(
        inside[..., None], jnp.exp(found_peak - new_max[:, None, :]) * found_sum, 0.0
    )
    added = jnp.sum(factor[..., None] * found_out, axis=1)
    numerator = numerator * jnp.repeat(rescale, HD, axis=1) + added.reshape(
        inst_rows, heads_here * HD
    )
    denominator = jnp.sum(factor, axis=1)
    running_max, numerator, denominator = (new_max, numerator, denominator)
    result = numerator.reshape(inst_rows, heads_here, HD) / denominator[..., None]
    finished = result.reshape(inst_rows, heads_here * HD).astype(jnp.bfloat16)
    return lax.all_to_all(finished, "tp", split_axis=0, concat_axis=1, tiled=True)


def solution(mesh):
    return jax.shard_map(
        per_device,
        mesh=mesh,
        in_specs=(P(("inst", "tp"), None), P(None, "inst", None, "tp"), P("inst", None), P("inst")),
        out_specs=P(("inst", "tp"), None),
        check_vma=False,
    )
```

profile of v0, /device:TPU:1, one launch (start us, length us, event | category | flops | bytes accessed | tf_op | source)
XLA Modules:
  0.0 355.4 jit_solution(3863443950831547460)
XLA Ops:
  6.5 0.6 broadcast.418
  7.1 1.5 reduce.8
  8.7 13.9 %all_to_all.29 = bf16[8,2,512]{2,1,0:T(2,128)(2,1)S(1)} all-to-all(bf16[8,2,512]{2,1,0:T(2,128)(2,1)S(1)} %reshape.386), channel_id=1, replica_groups=mesh['inst'=64,'tp'=8] {'tp'}, dimensions={0} | all-to-all | bytes 32768 | tf_op jit(solution)/shard_map/all_to_all | solution.py:15
  22.6 0.6 copy.53
  23.3 78.0 %all-gather.1 = s32[64,8,4]{1,2,0:T(4,128)S(1)} all-gather(s32[1,8,4]{1,2,0:T(4,128)} %bitcast.65), channel_id=1, replica_groups=mesh['inst'=64,'tp'=8] {'inst'}, dimensions={0}, use_global_device_ids=true | all-gather | bytes 8320 | tf_op jit(solution)/shard_map/all_gather | solution.py:18
  101.3 0.4 copy.52
  101.7 0.2 eq.17
  101.9 1.3 dynamic-slice
  104.0 0.9 dynamic-update-slice
  104.8 20.0 %all-reduce = s32[512]{0:T(512)S(1)} all-reduce(s32[512]{0:T(512)S(1)} %dynamic-update-slice), channel_id=1, replica_groups=mesh['inst'=64,'tp'=8] {'inst'}, use_global_device_ids=true, to_apply=%add | all-reduce | flops 512 | bytes 4096
  124.8 0.2 select_reduce_fusion
  125.1 0.7 gather_fusion
  125.9 26.0 %all-gather.9.cloned.1.call-done = bf16[1,512,1024]{2,1,0:T(8,128)(2,1)} async-done(((bf16[1,8,1024]{2,1,0:T(8,128)(2,1)}), bf16[1,512,1024]{2,1,0:T(8,128)(2,1)}) %all-gather.9.cloned.1.call-update) | async-done | bytes 1048592 | tf_op jit(solution)/shard_map/all_gather | solution.py:17
  151.9 2.0 gather_fusion.1
  153.9 0.1 bitcast_select_fusion
  154.1 2.3 fusion.31
  156.4 0.2 fusion.16
  156.7 2.0 fusion.12
  158.7 0.7 copy.68
  160.0 64.1 %all-gather.3 = f32[64,32,8]{1,2,0:T(8,128)S(1)} all-gather(f32[1,32,8]{1,2,0:T(8,128)S(1)} %copy.58), channel_id=1, replica_groups=mesh['inst'=64,'tp'=8] {'inst'}, dimensions={0}, use_global_device_ids=true | all-gather | bytes 66560 | tf_op jit(solution)/shard_map/all_gather | solution.py:67
  224.1 0.4 copy.59
  224.5 70.2 %all-gather.2 = f32[64,32,8]{1,2,0:T(8,128)S(1)} all-gather(f32[1,32,8]{1,2,0:T(8,128)S(1)} %copy.54), channel_id=1, replica_groups=mesh['inst'=64,'tp'=8] {'inst'}, dimensions={0}, use_global_device_ids=true | all-gather | bytes 66560 | tf_op jit(solution)/shard_map/all_gather | solution.py:66
  294.7 0.4 copy.55
  295.0 0.6 gather_fusion.4
  295.6 0.6 gather_fusion.3
  296.3 0.1 fusion.28
  296.4 19.1 %all-gather.7.cloned.1.call-done = f32[2048,1024]{1,0:T(8,128)} async-done(((f32[32,1024]{1,0:T(8,128)}), f32[2048,1024]{1,0:T(8,128)}) %all-gather.7.cloned.1.call-update) | async-done | bytes 8388624 | tf_op jit(solution)/shard_map/all_gather | solution.py:65
  315.5 4.1 %gather_fusion.2 = f32[32,1024]{1,0:T(8,128)S(1)} fusion(f32[2048,1024]{1,0:T(8,128)} %all-gather.7.cloned.1.call-done, s32[1024]{0:T(1024)S(1)} %pad_clamp_fusion), kind=kCustom, calls=%fused_computation.4 | custom fusion | bytes 262272 | tf_op jit(solution)/shard_map/jit(_take)/gather | solution.py:73
  319.6 0.1 multiply_reduce_fusion
  319.8 0.8 reduce.9
  320.6 27.3 %all_to_all.30 = bf16[8,2,512]{2,1,0:T(2,128)(2,1)S(1)} all-to-all(bf16[8,2,512]{2,1,0:T(2,128)(2,1)S(1)} %reshape.388), channel_id=1, replica_groups=mesh['inst'=64,'tp'=8] {'tp'}, dimensions={0} | all-to-all | bytes 32768 | tf_op jit(solution)/shard_map/all_to_all | solution.py:87
  347.9 0.6 reshape.389
  (34 shorter events, 1.1 us)
Async XLA Ops:
  6.5 145.4 %all-gather.9.cloned.1.call-start = ((), (), s32[]{:S(2)}) async-start(), calls=%async_computation.3 | async-start | bytes 1064960 | tf_op jit(solution)/shard_map/all_gather | solution.py:17
  23.2 136.2 %copy-start = (s32[8,4]{0,1:T(4,128)S(1)}, s32[8,4]{0,1:T(4,128)}, u32[]{:S(2)}) copy-start(s32[8,4]{0,1:T(4,128)} %param.8) | copy-start | bytes 388
  23.2 136.3 %copy-start.1 = (s32[8]{0:T(128)S(1)}, s32[8]{0:T(128)}, u32[]{:S(2)}) copy-start(s32[8]{0:T(128)} %param.9) | copy-start | bytes 100
  23.2 292.3 %all-gather.7.cloned.1.call-start = ((), (), s32[]{:S(2)}) async-start(), calls=%async_computation.2 | async-start | bytes 8519680 | tf_op jit(solution)/shard_map/all_gather | solution.py:65
Sparse Core Ops, SparseCore 0:
  23.3 128.5 all-gather.8
  159.5 155.9 all-gather.6
where the time goes:
time: 356 us; the launch traced here: 355 us
  blocking collectives  273 us (77%)
  waiting for transfers between devices  45.1 us (13%)
  local copies, waits for them, and re-layouts  14.6 us (4%)
  between operations  14.3 us (4%)
  matrix products  4.35 us (1%)
    all_gather x1, blocking collectives, per_device(): lax.all_gather(block_table, 'inst', axis=0, tiled=True)  78 us
    all_gather x1, blocking collectives, per_device(): piece_peak = lax.all_gather(block_peak, 'inst', axis=0, tiled=True)  70.2 us
    all_gather x1, blocking collectives, per_device(): piece_sum = lax.all_gather(block_sum, 'inst', axis=0, tiled=True)  64.1 us
    all_to_all x1, blocking collectives, per_device(): lax.all_to_all(finished, 'tp', split_axis=0, concat_axis=1, tiled=True)  27.3 us
    all_gather x1, waiting for transfers between devices, per_device(): lax.all_gather(local_query, 'inst', axis=0, tiled=True)  26 us
    unnamed x1, blocking collectives  20 us
    all_gather x1, waiting for transfers between devices, per_device(): piece_out = lax.all_gather(partial_value, 'inst', axis=0, tiled=True)  19.1 us
    all_to_all x1, blocking collectives, per_device(): lax.all_to_all(queries, 'tp', split_axis=1, concat_axis=0, tiled=True)  13.9 us
  transfers between devices with their start and end apart: 2, of which 2 were waited for; matrix products, arithmetic and copies ran while one was open for 2% of the time, Pallas kernels for 0%

commit v1 on v0

v1 whole, which is shorter than its diff:
```python
import functools
import math

import jax
import jax.numpy as jnp
from jax import lax
from jax.experimental import pallas as pl
from jax.experimental.pallas import tpu as pltpu
from jax.sharding import Mesh, PartitionSpec as P

HD = 128
NY = 4
TP = 8
GROUP = 8
MAXB = 4
BLK = 256
SLOTS = 32
ROWS = NY * TP
WIDE = GROUP * HD
LANES = WIDE + HD
NEG = -1e30
F32 = jnp.float32
BF16 = jnp.bfloat16


def dot(a, b, dims):
    return lax.dot_general(a, b, (dims, ((), ())), preferred_element_type=F32)


def split(x):
    hi = x.astype(BF16).astype(F32)
    mid = (x - hi).astype(BF16).astype(F32)
    return hi, mid, x - hi - mid


def lanes(shape):
    return lax.broadcasted_iota(jnp.int32, shape, len(shape) - 1)


def fan_kernel(me_ref, table_ref, len_ref, q_ref, out_ref):
    t = me_ref[0]
    lane = lanes((TP, GROUP, HD))
    extra = jnp.zeros((TP, GROUP, HD), F32)
    for b in range(MAXB):
        slot = table_ref[t, b]
        extra = jnp.where(lane == b, (slot // SLOTS).astype(F32), extra)
        extra = jnp.where(lane == MAXB + b, (slot % SLOTS).astype(F32), extra)
    length = len_ref[t]
    extra = jnp.where(lane == 8, (length // SLOTS).astype(F32), extra)
    extra = jnp.where(lane == 9, (length % SLOTS).astype(F32), extra)
    q = q_ref[...].astype(F32)
    heads = jnp.concatenate([q[:, h * HD : (h + 1) * HD] for h in range(TP * GROUP)], axis=0)
    both = jnp.concatenate([heads.reshape(TP, GROUP, HD), extra], axis=1).astype(BF16)
    for y in range(NY):
        out_ref[y * TP : (y + 1) * TP] = both


def pack_kernel(cap, me_ref, a_ref, out_ref, map_ref, scr):
    y = me_ref[1].astype(F32)
    targets = out_ref.shape[0]
    scr[...] = a_ref[...].reshape(ROWS * 16, HD).astype(F32)
    query = jnp.concatenate(
        [scr[pl.ds(g, ROWS, stride=16), :] for g in range(GROUP)], axis=1
    ).astype(BF16)
    extra = scr[pl.ds(GROUP, ROWS, stride=16), :]
    pool = jnp.concatenate([extra[:, b : b + 1] for b in range(MAXB)], axis=0)
    slot = jnp.concatenate([extra[:, MAXB + b : MAXB + b + 1] for b in range(MAXB)], axis=0)
    length = extra[:, 8:9] * SLOTS + extra[:, 9:10]
    filled = jnp.concatenate([length - b * BLK for b in range(MAXB)], axis=0)
    filled = jnp.clip(filled, 0.0, float(BLK))
    dest = jnp.floor(pool * (1.0 / NY))
    valid = (pool - dest * NY == y) & (filled > 0.0)
    entries = MAXB * ROWS
    lane = lanes((entries, HD)).astype(F32)
    member = jnp.where((lane == dest) & valid, 1.0, 0.0)
    earlier = jnp.where(
        lax.broadcasted_iota(jnp.int32, (entries, entries), 0) > lanes((entries, entries)), 1.0, 0.0
    ).astype(BF16)
    before = dot(earlier, member.astype(BF16), ((1,), (0,)))
    rank = jnp.sum(before * member, axis=1, keepdims=True)
    most = jnp.max(jnp.sum(member, axis=0, keepdims=True))
    target = jnp.where(valid & (rank < cap), dest * cap + rank, -1.0)
    place = jnp.where(lanes((entries, targets)).astype(F32) == target, 1.0, 0.0).astype(BF16)
    map_ref[...] = place
    lane = lanes((entries, HD))
    mine = jnp.where(lane == 0, slot + 1.0, jnp.where(lane == 1, filled, 0.0)).astype(BF16)
    four = jnp.concatenate([query] * MAXB, axis=0)
    out_ref[:, :WIDE] = dot(place, four, ((0,), (0,))).astype(BF16)
    extra = dot(place, mine, ((0,), (0,)))
    out_ref[:, WIDE:] = jnp.where(lanes((targets, HD)) == 2, most, extra).astype(BF16)


def attend_kernel(b_ref, kv_ref, out_ref, q_scr, f_scr, s_scr, p_scr, o_scr):
    targets = b_ref.shape[0]
    slot = b_ref[:, WIDE : WIDE + HD].astype(F32)[:, 0:1] - 1.0
    place = jnp.where(lanes((targets, SLOTS)).astype(F32) == slot, 1.0, 0.0).astype(BF16)
    got = dot(place, b_ref[...], ((0,), (0,)))
    for g in range(GROUP):
        rows = pl.ds(g, SLOTS, stride=GROUP)
        q_scr[rows, :] = got[:, g * HD : (g + 1) * HD]
        f_scr[rows, :] = jnp.broadcast_to(got[:, WIDE + 1 : WIDE + 2], (SLOTS, HD))
    for s in range(SLOTS):
        rows = slice(s * GROUP, (s + 1) * GROUP)
        s_scr[rows, :] = dot(q_scr[rows, :].astype(BF16), kv_ref[0, s], ((1,), (1,)))
    scores = s_scr[...] * (1.0 / math.sqrt(HD))
    mask = lanes((SLOTS * GROUP, BLK)).astype(F32) < f_scr[:, 0:1]
    scores = jnp.where(mask, scores, NEG)
    peak = jnp.max(scores, axis=1, keepdims=True)
    expo = jnp.where(mask, jnp.exp(scores - peak), 0.0)
    total = jnp.sum(expo, axis=1, keepdims=True)
    used = total > 0.0
    total = jnp.where(used, total, 1.0)
    p_scr[...] = expo
    for s in range(SLOTS):
        rows = slice(s * GROUP, (s + 1) * GROUP)
        o_scr[rows, :] = dot(p_scr[rows, :].astype(BF16), kv_ref[1, s], ((1,), (0,)))
    o_scr[...] = o_scr[...] / total
    level = jnp.where(used, peak + jnp.log(total), NEG)
    f_scr[...] = jnp.broadcast_to(level, (SLOTS * GROUP, HD))
    lane = lanes((SLOTS, HD))
    extra = jnp.zeros((SLOTS, HD), F32)
    parts = []
    for g in range(GROUP):
        rows = pl.ds(g, SLOTS, stride=GROUP)
        parts.append(o_scr[rows, :])
        for k, part in enumerate(split(f_scr[rows, :])):
            extra = jnp.where(lane == 3 * g + k, part, extra)
    back = jnp.concatenate(parts + [extra], axis=1).astype(BF16)
    out_ref[...] = dot(place, back, ((1,), (0,))).astype(BF16)


def gather_kernel(map_ref, c_ref, out_ref, scr):
    got, ok = [], []
    for b in range(MAXB):
        place = map_ref[b * ROWS : (b + 1) * ROWS, :]
        got.append(dot(place, c_ref[...], ((1,), (0,))))
        ok.append(jnp.sum(place.astype(F32), axis=1, keepdims=True) > 0.0)
    lane = lanes((ROWS, HD))
    for g in range(GROUP):
        level = []
        for b in range(MAXB):
            three = got[b][:, WIDE + 3 * g : WIDE + 3 * g + 3]
            level.append(jnp.where(ok[b], jnp.sum(three, axis=1, keepdims=True), NEG))
        top = functools.reduce(jnp.maximum, level)
        factor = [jnp.where(ok[b], jnp.exp(level[b] - top), 0.0) for b in range(MAXB)]
        total = functools.reduce(jnp.add, factor)
        any_ok = total > 0.0
        total = jnp.where(any_ok, total, 1.0)
        mixed = functools.reduce(
            jnp.add, [factor[b] * got[b][:, g * HD : (g + 1) * HD] for b in range(MAXB)]
        )
        scr[pl.ds(g, ROWS, stride=16), :] = mixed / total
        hi, mid, lo = split(jnp.where(any_ok, top + jnp.log(total), NEG))
        scr[pl.ds(GROUP + g, ROWS, stride=16), :] = jnp.where(
            lane == 0, hi, jnp.where(lane == 1, mid, jnp.where(lane == 2, lo, 0.0))
        )
    out_ref[...] = scr[...].reshape(ROWS, 16, HD).astype(BF16)


def finish_kernel(d_ref, out_ref):
    parts, level = [], []
    for y in range(NY):
        x = d_ref[y * TP : (y + 1) * TP].astype(F32)
        parts.append(x[:, :GROUP, :])
        level.append(jnp.sum(x[:, GROUP:, :], axis=2, keepdims=True))
    top = functools.reduce(jnp.maximum, level)
    factor = [jnp.exp(one - top) for one in level]
    total = functools.reduce(jnp.add, factor)
    mixed = functools.reduce(jnp.add, [f * p for f, p in zip(factor, parts)])
    result = (mixed / total).reshape(TP * GROUP, HD)
    out_ref[...] = jnp.concatenate(
        [result[h : h + 1, :] for h in range(TP * GROUP)], axis=1
    ).astype(BF16)


SMEM = pl.BlockSpec(memory_space=pltpu.SMEM)
VMEM = pl.BlockSpec(memory_space=pltpu.VMEM)


def call(kernel, out, ins, scratch=(), limit=32 << 20):
    return pl.pallas_call(
        kernel,
        out_shape=out,
        in_specs=ins,
        out_specs=jax.tree.map(lambda _: VMEM, out),
        scratch_shapes=scratch,
        compiler_params=pltpu.CompilerParams(vmem_limit_bytes=limit),
    )


def shape(dims, dtype=BF16):
    return jax.ShapeDtypeStruct(dims, dtype)


def per_device(cap, queries, kv_pool, block_table, lengths):
    nz = lax.axis_size("z")
    me = jnp.stack([lax.axis_index(("x", "c")), lax.axis_index("y")]).astype(jnp.int32)

    def over_plane(x):
        return lax.all_to_all(x, ("y", "x", "c"), 0, 0, tiled=True)

    def along_z(x, c):
        x = lax.all_to_all(x.reshape(nz, c, LANES), "z", 0, 0, tiled=True)
        return x.reshape(nz * c, LANES)

    def pack(rows, c):
        out, place = call(
            functools.partial(pack_kernel, c),
            (shape((nz * c, LANES)), shape((MAXB * ROWS, nz * c))),
            [SMEM, VMEM],
            [pltpu.VMEM((ROWS * 16, HD), F32)],
        )(me, rows)
        return along_z(out, c), place

    def attend(got, place, c):
        back = call(
            attend_kernel,
            shape((nz * c, LANES)),
            [VMEM, VMEM],
            [
                pltpu.VMEM((SLOTS * GROUP, HD), F32),
                pltpu.VMEM((SLOTS * GROUP, HD), F32),
                pltpu.VMEM((SLOTS * GROUP, BLK), F32),
                pltpu.VMEM((SLOTS * GROUP, BLK), F32),
                pltpu.VMEM((SLOTS * GROUP, HD), F32),
            ],
        )(got, kv_pool)
        return call(
            gather_kernel,
            shape((ROWS, 16, HD)),
            [VMEM, VMEM],
            [pltpu.VMEM((ROWS * 16, HD), F32)],
        )(place, along_z(back, c))

    fanned = call(fan_kernel, shape((ROWS, 16, HD)), [SMEM, SMEM, SMEM, VMEM])(
        me, block_table, lengths, queries
    )
    rows = over_plane(fanned)
    got, place = pack(rows, cap)
    most = jnp.max(got.reshape(nz, cap, LANES)[:, 0, WIDE + 2])
    mixed = lax.cond(
        most > cap,
        lambda: attend(*pack(rows, SLOTS), SLOTS),
        lambda: attend(got, place, cap),
    )
    return call(finish_kernel, shape((1, TP * WIDE)), [VMEM])(over_plane(mixed))


def solution(mesh):
    fine = Mesh(mesh.devices.reshape(-1, NY, TP // 2, 2), ("z", "y", "x", "c"))
    own = ("z", "y", "x", "c")
    return jax.shard_map(
        functools.partial(per_device, 8),
        mesh=fine,
        in_specs=(
            P(own, None),
            P(None, ("z", "y"), None, ("x", "c")),
            P(("z", "y"), None),
            P(("z", "y")),
        ),
        out_specs=P(own, None),
        check_vma=False,
    )
```

time: 356 us -> 100 us (0.28)
  blocking collectives: 273 us -> 59.4 us
  waiting for transfers between devices: 45.1 us -> 14.3 us
  starting transfers between devices: 0.04 us -> 13.7 us
  between operations: 14.3 us -> 0.69 us
  local copies, waits for them, and re-layouts: 14.6 us -> 2.17 us
  Pallas kernels: 0 us -> 8.88 us
  matrix products: 4.35 us -> 0 us
    all_gather x3 -> x0, blocking collectives: 212 us -> none  [the longest x1 78 us: per_device(): lax.all_gather(block_table, 'inst', axis=0, tiled=True)]
    all_gather x2 -> x0, waiting for transfers between devices: 45.1 us -> none  [the longest x1 26 us: per_device(): lax.all_gather(local_query, 'inst', axis=0, tiled=True)]
    unnamed x1 -> x0, blocking collectives: 20 us -> none
    all_to_all x2 -> x3, blocking collectives: 41.2 us -> 59.4 us  [the longest x2 34.2 us: over_plane(): return lax.all_to_all(x, ('y', 'x', 'c'), 0, 0, tiled=True)]
    all_to_all x0 -> x1, waiting for transfers between devices: none -> 14.3 us  [along_z(): x = lax.all_to_all(x.reshape(nz, c, LANES), 'z', 0, 0, tiled=True)]
    all_to_all x0 -> x1, starting transfers between devices: none -> 13.7 us  [along_z(): x = lax.all_to_all(x.reshape(nz, c, LANES), 'z', 0, 0, tiled=True)]
    pallas_call x0 -> x5, Pallas kernels: none -> 8.88 us  [the longest x1 3.6 us: attend(): call(attend_kernel, shape((nz * c, LANES)), [VMEM, VMEM], [pltpu.VMEM((SL...]
    gather x5 -> x0, local copies, waits for them, and re-layouts: 7.95 us -> none  [the longest x1 4.05 us: per_device(): jnp.take(piece_out, position, axis=0)]
  transfers between devices with their start and end apart: 2 -> 1, of which waited for: 2 -> 1; matrix products, arithmetic and copies ran while one was open for 2% -> 0% of each run, Pallas kernels for 0% -> 0%
where the time goes in v1:
time: 100 us; the launch traced here: 99.9 us
  blocking collectives  59.4 us (59%)
  waiting for transfers between devices  14.3 us (14%)
  starting transfers between devices  13.7 us (14%)
  Pallas kernels  8.88 us (9%)
  local copies, waits for them, and re-layouts  2.17 us (2%)
    all_to_all x2, blocking collectives, over_plane(): return lax.all_to_all(x, ('y', 'x', 'c'), 0, 0, tiled=True)  34.2 us
    all_to_all x1, blocking collectives, along_z(): x = lax.all_to_all(x.reshape(nz, c, LANES), 'z', 0, 0, tiled=True)  25.2 us
    all_to_all x1, waiting for transfers between devices, along_z(): x = lax.all_to_all(x.reshape(nz, c, LANES), 'z', 0, 0, tiled=True)  14.3 us
    all_to_all x1, starting transfers between devices, along_z(): x = lax.all_to_all(x.reshape(nz, c, LANES), 'z', 0, 0, tiled=True)  13.7 us
    pallas_call x1, Pallas kernels, attend(): call(attend_kernel, shape((nz * c, LANES)), [VMEM, VMEM], [pltpu.VMEM((SL...  3.6 us
    unnamed x5, local copies, waits for them, and re-layouts  2.17 us
    pallas_call x1, Pallas kernels, pack(): call(functools.partial(pack_kernel, c), (shape((nz * c, LANES)), shape((M...  2.03 us
  transfers between devices with their start and end apart: 1, of which 1 were waited for; matrix products, arithmetic and copies ran while one was open for 0% of the time, Pallas kernels for 0%

profile of v1, /device:TPU:1, one launch (start us, length us, event | category | flops | bytes accessed | tf_op | source)
XLA Modules:
  0.0 99.9 jit_solution(2787944382162246769)
XLA Ops:
  0.0 0.8 copy.5.table_ref
  0.8 0.1 pad_add_fusion.me_ref
  0.8 0.0 copy-start
  0.8 0.8 copy-done
  1.6 0.0 copy-start.1
  1.6 0.7 copy-done.1
  2.2 0.7 shard_map.46
  2.9 17.2 %all_to_all.30.a_ref = bf16[32,16,128]{2,1,0:T(8,128)(2,1)S(1)} all-to-all(bf16[32,16,128]{2,1,0:T(8,128)(2,1)S(1)} %shard_map.46), channel_id=1, replica_groups=mesh['z'=16,'y'=4,'x'=4,'c'=2] {'y','x','c'}, dimensions={0} | all-to-all | bytes 262144 | tf_op jit(solution)/shard_map/all_to_all | solution.py:200
  20.2 2.0 %shard_map.47 = (bf16[128,1152]{1,0:T(8,128)(2,1)}, bf16[128,128]{1,0:T(8,128)(2,1)S(1)}) custom-call(s32[2]{0:T(128)S(1)} %pad_add_fusion.me_ref, bf16[32,16,128]{2,1,0:T(8,128)(2,1)S(1)} %all_to_all.30.a_ref), custom_call_target="tpu_custom_call" | custom-call | tf_op jit(solution)/shard_map/pallas_call | solution.py:207
  22.2 13.7 %all-to-all-start.4 = ((bf16[16,8,1152]{2,1,0:T(8,128)(2,1)}), bf16[16,8,1152]{2,1,0:T(8,128)(2,1)S(1)}, u32[]{:S(2)}, u32[]{:S(2)}) async-start(bf16[16,8,1152]{2,1,0:T(8,128)(2,1)} %bitcast.9), calls=%async_computation.4 | async-start | bytes 589824 | tf_op jit(solution)/shard_map/all_to_all | solution.py:203
  35.9 14.3 %all-to-all-done.4 = bf16[16,8,1152]{2,1,0:T(8,128)(2,1)S(1)} async-done(((bf16[16,8,1152]{2,1,0:T(8,128)(2,1)}), bf16[16,8,1152]{2,1,0:T(8,128)(2,1)S(1)}, u32[]{:S(2)}, u32[]{:S(2)}) %all-to-all-start.4) | async-done | bytes 294944 | tf_op jit(solution)/shard_map/all_to_all | solution.py:203
  50.2 0.7 slice_reduce_fusion
  51.5 30.7 %conditional.1 = (bf16[32,16,128]{2,1,0:T(8,128)(2,1)S(1)}) conditional(s32[]{:T(128)} %convert_element_type.3, (bf16[16,8,1152]{2,1,0:T(8,128)(2,1)S(1)}, bf16[2,32,256,128]{3,2,1,0:T(8,128)(2,1)}, bf16[128,128]{1,0:T(8,128)(2,1)S(1)}) %tuple.11, (s32[2]{0:T(128)S(1)}, bf16[32,16,128]{2,1,0:T(8,128)(2,1)S(1)}, ...), branch_computations={%region_1.0_spmd, %region_2.0_spmd} | conditional | bytes 4718600 | solution.py:241
  51.6 3.6 %branch_0_fun.2 = bf16[128,1152]{1,0:T(8,128)(2,1)S(1)} custom-call(bf16[128,1152]{1,0:T(8,128)(2,1)S(1)} %bitcast.16, bf16[2,32,256,128]{3,2,1,0:T(8,128)(2,1)} %get-tuple-element.23.kv_ref), custom_call_target="tpu_custom_call" | custom-call | tf_op jit(solution)/shard_map/cond/branch_0_fun/pallas_call | solution.py:216
  55.2 25.2 %all_to_all.27 = bf16[16,8,1152]{2,1,0:T(8,128)(2,1)S(1)} all-to-all(bf16[16,8,1152]{2,1,0:T(8,128)(2,1)S(1)} %bitcast.13), channel_id=1, replica_groups=mesh['z'=16,'y'=4,'x'=4,'c'=2] {'z'}, dimensions={0} | all-to-all | bytes 589824 | tf_op jit(solution)/shard_map/cond/branch_0_fun/all_to_all | solution.py:203
  80.4 1.8 %branch_0_fun.3 = bf16[32,16,128]{2,1,0:T(8,128)(2,1)S(1)} custom-call(bf16[128,128]{1,0:T(8,128)(2,1)S(1)} %get-tuple-element.21.map_ref, bf16[128,1152]{1,0:T(8,128)(2,1)S(1)} %bitcast.15), custom_call_target="tpu_custom_call" | custom-call | tf_op jit(solution)/shard_map/cond/branch_0_fun/pallas_call | solution.py:228
  82.2 16.9 %all_to_all.31.d_ref = bf16[32,16,128]{2,1,0:T(8,128)(2,1)S(1)} all-to-all(bf16[32,16,128]{2,1,0:T(8,128)(2,1)S(1)} %get-tuple-element.33), channel_id=1, replica_groups=mesh['z'=16,'y'=4,'x'=4,'c'=2] {'y','x','c'}, dimensions={0} | all-to-all | bytes 262144 | tf_op jit(solution)/shard_map/all_to_all | solution.py:200
  99.2 0.8 shard_map.48
Async XLA Ops:
  0.8 0.8 copy-start
  1.6 0.7 copy-start.1
  22.2 28.0 %all-to-all-start.4 = ((bf16[16,8,1152]{2,1,0:T(8,128)(2,1)}), bf16[16,8,1152]{2,1,0:T(8,128)(2,1)S(1)}, u32[]{:S(2)}, u32[]{:S(2)}) async-start(bf16[16,8,1152]{2,1,0:T(8,128)(2,1)} %bitcast.9), calls=%async_computation.4 | async-start | bytes 589824 | tf_op jit(solution)/shard_map/all_to_all | solution.py:203

commit v2 on v1

v2 whole, which is shorter than its diff:
```python
import functools
import math

import jax
import jax.numpy as jnp
from jax import lax
from jax.experimental import pallas as pl
from jax.experimental.pallas import tpu as pltpu
from jax.sharding import Mesh, PartitionSpec as P

HD = 128
NY = 4
TP = 8
GROUP = 8
MAXB = 4
BLK = 256
SLOTS = 32
ROWS = NY * TP
WIDE = GROUP * HD
NEG = -1e30
F32 = jnp.float32
BF16 = jnp.bfloat16


def dot(a, b, dims):
    return lax.dot_general(a, b, (dims, ((), ())), preferred_element_type=F32)


def split(x):
    hi = x.astype(BF16).astype(F32)
    mid = (x - hi).astype(BF16).astype(F32)
    return hi, mid, x - hi - mid


def lanes(shape):
    return lax.broadcasted_iota(jnp.int32, shape, len(shape) - 1)


def fan_kernel(q_hbm, table_hbm, len_hbm, out_ref, q_ref, table_ref, len_ref, sems):
    copies = [
        pltpu.make_async_copy(q_hbm, q_ref, sems.at[0]),
        pltpu.make_async_copy(table_hbm, table_ref, sems.at[1]),
        pltpu.make_async_copy(len_hbm, len_ref, sems.at[2]),
    ]
    for copy in copies:
        copy.start()
    for copy in copies:
        copy.wait()
    t = lax.axis_index("x") * 2 + lax.axis_index("c")
    lane = lanes((TP, GROUP, HD))
    extra = jnp.zeros((TP, GROUP, HD), F32)
    for b in range(MAXB):
        slot = table_ref[b, t]
        extra = jnp.where(lane == b, (slot // SLOTS).astype(F32), extra)
        extra = jnp.where(lane == MAXB + b, (slot % SLOTS).astype(F32), extra)
    length = len_ref[t]
    extra = jnp.where(lane == 8, (length // SLOTS).astype(F32), extra)
    extra = jnp.where(lane == 9, (length % SLOTS).astype(F32), extra)
    q = q_ref[...].astype(F32)
    heads = jnp.concatenate([q[:, h * HD : (h + 1) * HD] for h in range(TP * GROUP)], axis=0)
    both = jnp.concatenate([heads.reshape(TP, GROUP, HD), extra], axis=1).astype(BF16)
    for y in range(NY):
        out_ref[y * TP : (y + 1) * TP] = both


def pack_kernel(cap, skip, a_ref, out_ref, map_ref, scr):
    y = lax.axis_index("y").astype(F32)
    targets = out_ref.shape[0]
    tall = cap + 1
    scr[...] = a_ref[...].reshape(ROWS * 16, HD).astype(F32)
    query = jnp.concatenate(
        [scr[pl.ds(g, ROWS, stride=16), :] for g in range(GROUP)], axis=1
    ).astype(BF16)
    extra = scr[pl.ds(GROUP, ROWS, stride=16), :]
    pool = jnp.concatenate([extra[:, b : b + 1] for b in range(MAXB)], axis=0)
    slot = jnp.concatenate([extra[:, MAXB + b : MAXB + b + 1] for b in range(MAXB)], axis=0)
    length = extra[:, 8:9] * SLOTS + extra[:, 9:10]
    filled = jnp.concatenate([length - b * BLK for b in range(MAXB)], axis=0)
    filled = jnp.clip(filled, 0.0, float(BLK))
    dest = jnp.floor(pool * (1.0 / NY))
    valid = (pool - dest * NY == y) & (filled > 0.0)
    entries = MAXB * ROWS
    lane = lanes((entries, HD))
    member = jnp.where((lane.astype(F32) == dest) & valid, 1.0, 0.0)
    earlier = jnp.where(
        lax.broadcasted_iota(jnp.int32, (entries, entries), 0) > lanes((entries, entries)), 1.0, 0.0
    ).astype(BF16)
    before = dot(earlier, member.astype(BF16), ((1,), (0,)))
    rank = jnp.sum(before * member, axis=1, keepdims=True)
    most = jnp.max(jnp.sum(member, axis=0, keepdims=True))
    rank = rank - skip
    fits = valid & (rank >= 0.0) & (rank < cap)
    column = lanes((entries, targets)).astype(F32)
    place = jnp.where(column == jnp.where(fits, dest * tall + rank, -1.0), 1.0, 0.0).astype(BF16)
    last = jnp.where(column == jnp.where(fits, dest * tall + cap, -1.0), 1.0, 0.0).astype(BF16)
    map_ref[...] = place
    mine = jnp.where(lane % 2 == 0, slot + 1.0, filled)
    mine = jnp.where((lane // 2).astype(F32) == rank, mine, 0.0).astype(BF16)
    four = jnp.concatenate([query] * MAXB, axis=0)
    out_ref[...] = dot(place, four, ((0,), (0,))).astype(BF16)
    numbers = dot(last, mine, ((0,), (0,)))
    numbers = jnp.where(lanes((targets, HD)) == 2 * cap, most, numbers)
    final = lax.broadcasted_iota(jnp.int32, (targets, HD), 0) % tall == cap
    head = out_ref[:, :HD].astype(F32)
    out_ref[:, :HD] = jnp.where(final, numbers, head).astype(BF16)


def own_lanes(x, tall, width):
    groups = x.shape[0] // tall
    x = x.astype(F32).reshape(groups, tall, HD)
    last = jnp.broadcast_to(x[:, tall - 1 : tall, :], (groups, tall, HD))
    row = lax.broadcasted_iota(jnp.int32, (groups, tall, HD), 1)
    mine = (lanes((groups, tall, HD)) // width == row) & (row < tall - 1)
    return jnp.where(mine, last, 0.0).reshape(groups * tall, HD)


def attend_kernel(cap, b_ref, kv_ref, out_ref, most_ref, q_scr, f_scr, s_scr, p_scr, o_scr):
    targets = b_ref.shape[0]
    tall = cap + 1
    numbers = b_ref[:, :HD]
    lane = lanes((targets, HD))
    row = lax.broadcasted_iota(jnp.int32, (targets, HD), 0)
    most = jnp.max(
        jnp.where((row % tall == cap) & (lane == 2 * cap), numbers.astype(F32), 0.0)
    )
    most_ref[0] = jnp.where(most > 2 * cap, 2, jnp.where(most > cap, 1, 0))
    own = own_lanes(numbers, tall, 2)
    slot = jnp.sum(jnp.where(lane % 2 == 0, own, 0.0), axis=1, keepdims=True) - 1.0
    filled = jnp.sum(jnp.where(lane % 2 == 1, own, 0.0), axis=1, keepdims=True)
    place = jnp.where(lanes((targets, SLOTS)).astype(F32) == slot, 1.0, 0.0).astype(BF16)
    got = dot(place, b_ref[...], ((0,), (0,)))
    filled = jnp.broadcast_to(filled, (targets, HD)).astype(BF16)
    filled = dot(place, filled, ((0,), (0,)))
    for g in range(GROUP):
        rows = pl.ds(g, SLOTS, stride=GROUP)
        q_scr[rows, :] = got[:, g * HD : (g + 1) * HD]
        f_scr[rows, :] = filled
    for s in range(SLOTS):
        rows = slice(s * GROUP, (s + 1) * GROUP)
        s_scr[rows, :] = dot(q_scr[rows, :].astype(BF16), kv_ref[0, s], ((1,), (1,)))
    scores = s_scr[...] * (1.0 / math.sqrt(HD))
    mask = lanes((SLOTS * GROUP, BLK)).astype(F32) < f_scr[:, 0:1]
    scores = jnp.where(mask, scores, NEG)
    peak = jnp.max(scores, axis=1, keepdims=True)
    expo = jnp.where(mask, jnp.exp(scores - peak), 0.0)
    total = jnp.sum(expo, axis=1, keepdims=True)
    used = total > 0.0
    total = jnp.where(used, total, 1.0)
    p_scr[...] = expo
    for s in range(SLOTS):
        rows = slice(s * GROUP, (s + 1) * GROUP)
        o_scr[rows, :] = dot(p_scr[rows, :].astype(BF16), kv_ref[1, s], ((1,), (0,)))
    o_scr[...] = o_scr[...] / total
    level = jnp.where(used, peak + jnp.log(total), NEG)
    f_scr[...] = jnp.broadcast_to(level, (SLOTS * GROUP, HD))
    lane = lanes((SLOTS, HD)) % 16
    coarse = jnp.zeros((SLOTS, HD), F32)
    fine = jnp.zeros((SLOTS, HD), F32)
    parts = []
    for g in range(GROUP):
        rows = pl.ds(g, SLOTS, stride=GROUP)
        parts.append(o_scr[rows, :])
        hi, mid, lo = split(f_scr[rows, :])
        coarse = jnp.where(lane == 2 * g, hi, jnp.where(lane == 2 * g + 1, mid, coarse))
        fine = jnp.where(lane == 2 * g, lo, fine)
    back = jnp.concatenate(parts, axis=1).astype(BF16)
    out_ref[...] = dot(place, back, ((1,), (0,))).astype(BF16)
    final = row % tall == cap
    lane = lanes((targets, HD))
    for k, part in enumerate((coarse, fine)):
        each = dot(place, part.astype(BF16), ((1,), (0,)))
        each = jnp.where(lane // 16 == row % tall, each, 0.0).reshape(targets // tall, tall, HD)
        both = jnp.broadcast_to(jnp.sum(each, axis=1, keepdims=True), each.shape)
        spot = slice(k * HD, (k + 1) * HD)
        head = out_ref[:, spot].astype(F32)
        out_ref[:, spot] = jnp.where(final, both.reshape(targets, HD), head).astype(BF16)


def gather_kernel(cap, map_ref, c_ref, out_ref, scr):
    tall = cap + 1
    coarse = own_lanes(c_ref[:, :HD], tall, 16).astype(BF16)
    fine = own_lanes(c_ref[:, HD : 2 * HD], tall, 16).astype(BF16)
    pick = lax.broadcasted_iota(jnp.int32, (HD, HD), 0) % 16 // 2 == lanes((HD, HD))
    pick = jnp.where(pick, 1.0, 0.0).astype(BF16)
    got, ok, levels = [], [], []
    for b in range(MAXB):
        place = map_ref[b * ROWS : (b + 1) * ROWS, :]
        got.append(dot(place, c_ref[...], ((1,), (0,))))
        ok.append(jnp.sum(place.astype(F32), axis=1, keepdims=True) > 0.0)
        level = 0.0
        for part in (coarse, fine):
            part = dot(place, part, ((1,), (0,))).astype(BF16)
            level = level + dot(part, pick, ((1,), (0,)))
        levels.append(level)
    lane = lanes((ROWS, HD))
    top = functools.reduce(
        jnp.maximum, [jnp.where(o, level, NEG) for o, level in zip(ok, levels)]
    )
    factor = [jnp.where(o, jnp.exp(level - top), 0.0) for o, level in zip(ok, levels)]
    total = functools.reduce(jnp.add, factor)
    any_ok = total > 0.0
    total = jnp.where(any_ok, total, 1.0)
    three = split(jnp.where(any_ok, top + jnp.log(total), NEG))
    factor = [f / total for f in factor]
    for g in range(GROUP):
        mixed = functools.reduce(
            jnp.add,
            [factor[b][:, g : g + 1] * got[b][:, g * HD : (g + 1) * HD] for b in range(MAXB)],
        )
        scr[pl.ds(g, ROWS, stride=16), :] = mixed
        hi, mid, lo = [part[:, g : g + 1] for part in three]
        scr[pl.ds(GROUP + g, ROWS, stride=16), :] = jnp.where(
            lane == 0, hi, jnp.where(lane == 1, mid, jnp.where(lane == 2, lo, 0.0))
        )
    out_ref[...] = scr[...].reshape(ROWS, 16, HD).astype(BF16)


def finish_kernel(d_ref, out_ref):
    parts, level = [], []
    for y in range(NY):
        x = d_ref[y * TP : (y + 1) * TP].astype(F32)
        parts.append(x[:, :GROUP, :])
        level.append(jnp.sum(x[:, GROUP:, :], axis=2, keepdims=True))
    top = functools.reduce(jnp.maximum, level)
    factor = [jnp.exp(one - top) for one in level]
    total = functools.reduce(jnp.add, factor)
    mixed = functools.reduce(jnp.add, [f * p for f, p in zip(factor, parts)])
    result = (mixed / total).reshape(TP * GROUP, HD)
    out_ref[...] = jnp.concatenate(
        [result[h : h + 1, :] for h in range(TP * GROUP)], axis=1
    ).astype(BF16)


SMEM = pl.BlockSpec(memory_space=pltpu.SMEM)
VMEM = pl.BlockSpec(memory_space=pltpu.VMEM)
HBM = pl.BlockSpec(memory_space=pltpu.HBM)


def call(kernel, out, ins, scratch=(), outs=VMEM, limit=24 << 20):
    return pl.pallas_call(
        kernel,
        out_shape=out,
        in_specs=ins,
        out_specs=outs,
        scratch_shapes=scratch,
        compiler_params=pltpu.CompilerParams(vmem_limit_bytes=limit),
    )


def shape(*dims):
    return jax.ShapeDtypeStruct(dims, BF16)


def per_device(cap, queries, kv_pool, block_table, lengths):
    nz = lax.axis_size("z")
    targets = nz * (cap + 1)

    def over_plane(x):
        return lax.all_to_all(x, ("y", "x", "c"), 0, 0, tiled=True)

    def along_z(x):
        x = lax.all_to_all(x.reshape(nz, -1, WIDE), "z", 0, 0, tiled=True)
        return x.reshape(-1, WIDE)

    def pack(rows, skip):
        return call(
            functools.partial(pack_kernel, cap, skip),
            (shape(targets, WIDE), shape(MAXB * ROWS, targets)),
            [VMEM],
            [pltpu.VMEM((ROWS * 16, HD), F32)],
            (VMEM, VMEM),
        )(rows)

    def attend(got, kv):
        return call(
            functools.partial(attend_kernel, cap),
            (shape(targets, WIDE), jax.ShapeDtypeStruct((1,), jnp.int32)),
            [VMEM, VMEM],
            [
                pltpu.VMEM((SLOTS * GROUP, HD), F32),
                pltpu.VMEM((SLOTS * GROUP, HD), F32),
                pltpu.VMEM((SLOTS * GROUP, BLK), F32),
                pltpu.VMEM((SLOTS * GROUP, BLK), F32),
                pltpu.VMEM((SLOTS * GROUP, HD), F32),
            ],
            (VMEM, SMEM),
        )(got, kv)

    def gather(places, backs):
        backs = [along_z(back) for back in backs]
        return call(
            functools.partial(gather_kernel, cap),
            shape(ROWS, 16, HD),
            [VMEM, VMEM],
            [pltpu.VMEM((ROWS * 16, HD), F32)],
        )(jnp.concatenate(places, axis=1), jnp.concatenate(backs, axis=0))

    def rounds(count):
        places, backs = [place], [back]
        for k in range(1, count):
            out, more = pack(rows, k * cap)
            places.append(more)
            backs.append(attend(along_z(out), kv_pool)[0])
        return gather(places, backs)

    fanned = call(
        fan_kernel,
        shape(ROWS, 16, HD),
        [HBM, HBM, HBM],
        [
            pltpu.VMEM((1, TP * WIDE), BF16),
            pltpu.SMEM((MAXB, TP), jnp.int32),
            pltpu.SMEM((TP,), jnp.int32),
            pltpu.SemaphoreType.DMA((3,)),
        ],
    )(queries, block_table.T, lengths)
    rows = over_plane(fanned)
    out, place = pack(rows, 0)
    got = along_z(out)
    got, place, rows, kv_pool = lax.optimization_barrier((got, place, rows, kv_pool))
    back, over = attend(got, kv_pool)
    mixed = lax.switch(
        over[0], [lambda: rounds(1), lambda: rounds(2), lambda: rounds(-(-SLOTS // cap))]
    )
    return call(finish_kernel, shape(1, TP * WIDE), [VMEM])(over_plane(mixed))


def solution(mesh):
    fine = Mesh(mesh.devices.reshape(-1, NY, TP // 2, 2), ("z", "y", "x", "c"))
    own = ("z", "y", "x", "c")
    return jax.shard_map(
        functools.partial(per_device, 7),
        mesh=fine,
        in_specs=(
            P(own, None),
            P(None, ("z", "y"), None, ("x", "c")),
            P(("z", "y"), None),
            P(("z", "y")),
        ),
        out_specs=P(own, None),
        check_vma=False,
    )
```

time: 100 us -> 96.1 us (0.961)
  blocking collectives: 59.4 us -> 84.9 us
  waiting for transfers between devices: 14.3 us -> 0 us
  starting transfers between devices: 13.7 us -> 0 us
  Pallas kernels: 8.88 us -> 7.72 us
    all_to_all x1 -> x2, blocking collectives: 25.2 us -> 51.2 us  [along_z(): x = lax.all_to_all(x.reshape(nz, -1, WIDE), 'z', 0, 0, tiled=True)]
    all_to_all x1 -> x0, waiting for transfers between devices: 14.3 us -> none  [along_z(): x = lax.all_to_all(x.reshape(nz, c, LANES), 'z', 0, 0, tiled=True)]
    all_to_all x1 -> x0, starting transfers between devices: 13.7 us -> none  [along_z(): x = lax.all_to_all(x.reshape(nz, c, LANES), 'z', 0, 0, tiled=True)]
    pallas_call x5, Pallas kernels: 8.88 us -> 7.72 us  [the longest x1 4.36 us: attend(): call(functools.partial(attend_kernel, cap), (shape(targets, WIDE), jax.Sh...]
    unnamed x5 -> x6, local copies, waits for them, and re-layouts: 2.17 us -> 2.09 us
  transfers between devices with their start and end apart: 1 -> 0, of which waited for: 1 -> 0; matrix products, arithmetic and copies ran while one was open for 0% -> 0% of each run, Pallas kernels for 0% -> 0%
where the time goes in v2:
time: 96.1 us; the launch traced here: 95.6 us
  blocking collectives  84.9 us (88%)
  Pallas kernels  7.72 us (8%)
  local copies, waits for them, and re-layouts  2.09 us (2%)
    all_to_all x2, blocking collectives, along_z(): x = lax.all_to_all(x.reshape(nz, -1, WIDE), 'z', 0, 0, tiled=True)  51.2 us
    all_to_all x2, blocking collectives, over_plane(): return lax.all_to_all(x, ('y', 'x', 'c'), 0, 0, tiled=True)  33.7 us
    pallas_call x1, Pallas kernels, attend(): call(functools.partial(attend_kernel, cap), (shape(targets, WIDE), jax.Sh...  4.36 us
    unnamed x6, local copies, waits for them, and re-layouts  2.09 us

profile of v2, /device:TPU:1, one launch (start us, length us, event | category | flops | bytes accessed | tf_op | source)
XLA Modules:
  0.0 95.6 jit_solution(2820144409842702586)
XLA Ops:
  0.0 0.0 copy-start
  0.0 0.8 copy-done
  0.8 0.0 copy-start.1
  0.8 0.7 copy-done.1
  1.4 0.0 copy-start.2
  1.4 0.7 copy-done.2
  2.1 0.7 shard_map.46
  2.8 17.2 %all_to_all.70.a_ref = bf16[32,16,128]{2,1,0:T(8,128)(2,1)S(1)} all-to-all(bf16[32,16,128]{2,1,0:T(8,128)(2,1)S(1)} %shard_map.46), channel_id=1, replica_groups=mesh['z'=16,'y'=4,'x'=4,'c'=2] {'y','x','c'}, dimensions={0} | all-to-all | bytes 262144 | tf_op jit(solution)/shard_map/all_to_all | solution.py:259
  20.0 0.8 shard_map.47
  20.8 27.4 %all_to_all.71 = bf16[16,8,1024]{2,1,0:T(8,128)(2,1)S(1)} all-to-all(bf16[16,8,1024]{2,1,0:T(8,128)(2,1)S(1)} %bitcast.42), channel_id=1, replica_groups=mesh['z'=16,'y'=4,'x'=4,'c'=2] {'z'}, dimensions={0} | all-to-all | bytes 524288 | tf_op jit(solution)/shard_map/all_to_all | solution.py:262
  48.2 4.4 %shard_map.48 = (bf16[128,1024]{1,0:T(8,128)(2,1)}, s32[1]{0:T(128)}) custom-call(bf16[128,1024]{1,0:T(8,128)(2,1)S(1)} %bitcast.40, bf16[2,32,256,128]{3,2,1,0:T(8,128)(2,1)} %kv_ref), custom_call_target="tpu_custom_call" | custom-call | tf_op jit(solution)/shard_map/pallas_call | solution.py:275
  53.2 25.2 %conditional.1 = (bf16[32,16,128]{2,1,0:T(8,128)(2,1)S(1)}) conditional(s32[]{:T(128)} %bitcast.29, (bf16[128,1024]{1,0:T(8,128)(2,1)}, bf16[128,128]{1,0:T(8,128)(2,1)S(1)}) %tuple.16, (bf16[32,16,128]{2,1,0:T(8,128)(2,1)S(1)}, bf16[128,128]{1,0:T(8,128)(2,1)S(1)}, bf16[128,1024]{1,0:T(8,128)(2,1)}, ...), branch_computations={%region_0.0_spmd, %region_1.0_spmd, %region_2.0_spmd} | conditional | flops 1179648 | bytes 9765128 | solution.py:322
  53.2 23.8 %all_to_all.67 = bf16[16,8,1024]{2,1,0:T(8,128)(2,1)S(1)} all-to-all(bf16[16,8,1024]{2,1,0:T(8,128)(2,1)} %bitcast), channel_id=1, replica_groups=mesh['z'=16,'y'=4,'x'=4,'c'=2] {'z'}, dimensions={0} | all-to-all | bytes 524288 | tf_op jit(solution)/shard_map/cond/branch_0_fun/all_to_all | solution.py:262
  77.0 1.1 %branch_0_fun.1 = bf16[32,16,128]{2,1,0:T(8,128)(2,1)S(1)} custom-call(bf16[128,128]{1,0:T(8,128)(2,1)S(1)} %get-tuple-element.28.map_ref, bf16[128,1024]{1,0:T(8,128)(2,1)S(1)} %bitcast.41), custom_call_target="tpu_custom_call" | custom-call | tf_op jit(solution)/shard_map/cond/branch_0_fun/pallas_call | solution.py:291
  78.4 16.5 %all_to_all.72.d_ref = bf16[32,16,128]{2,1,0:T(8,128)(2,1)S(1)} all-to-all(bf16[32,16,128]{2,1,0:T(8,128)(2,1)S(1)} %get-tuple-element.70), channel_id=1, replica_groups=mesh['z'=16,'y'=4,'x'=4,'c'=2] {'y','x','c'}, dimensions={0} | all-to-all | bytes 262144 | tf_op jit(solution)/shard_map/all_to_all | solution.py:259
  94.9 0.8 shard_map.49
Async XLA Ops:
  0.0 0.8 copy-start
  0.8 0.7 copy-start.1
  1.4 0.7 copy-start.2

commit v3 on v2

--- a/solution.py
+++ b/solution.py
@@ -63,7 +63,7 @@
         out_ref[y * TP : (y + 1) * TP] = both
 
 
-def pack_kernel(cap, skip, a_ref, out_ref, map_ref, scr):
+def pack_kernel(cap, skip, a_ref, kv_hbm, out_ref, map_ref, scr):
     y = lax.axis_index("y").astype(F32)
     targets = out_ref.shape[0]
     tall = cap + 1
@@ -266,12 +266,12 @@
         return call(
             functools.partial(pack_kernel, cap, skip),
             (shape(targets, WIDE), shape(MAXB * ROWS, targets)),
-            [VMEM],
+            [VMEM, HBM],
             [pltpu.VMEM((ROWS * 16, HD), F32)],
             (VMEM, VMEM),
-        )(rows)
-
-    def attend(got, kv):
+        )(rows, kv_pool)
+
+    def attend(got):
         return call(
             functools.partial(attend_kernel, cap),
             (shape(targets, WIDE), jax.ShapeDtypeStruct((1,), jnp.int32)),
@@ -284,10 +284,9 @@
                 pltpu.VMEM((SLOTS * GROUP, HD), F32),
             ],
             (VMEM, SMEM),
-        )(got, kv)
+        )(got, kv_pool)
 
     def gather(places, backs):
-        backs = [along_z(back) for back in backs]
         return call(
             functools.partial(gather_kernel, cap),
             shape(ROWS, 16, HD),
@@ -300,7 +299,7 @@
         for k in range(1, count):
             out, more = pack(rows, k * cap)
             places.append(more)
-            backs.append(attend(along_z(out), kv_pool)[0])
+            backs.append(along_z(attend(along_z(out))[0]))
         return gather(places, backs)
 
     fanned = call(
@@ -313,14 +312,18 @@
             pltpu.SMEM((TP,), jnp.int32),
             pltpu.SemaphoreType.DMA((3,)),
         ],
+        limit=60 << 20,
     )(queries, block_table.T, lengths)
     rows = over_plane(fanned)
     out, place = pack(rows, 0)
     got = along_z(out)
     got, place, rows, kv_pool = lax.optimization_barrier((got, place, rows, kv_pool))
-    back, over = attend(got, kv_pool)
+    back, over = attend(got)
+    back = along_z(back)
+    back, place, rows, over, kv_pool = lax.optimization_barrier((back, place, rows, over, kv_pool))
+    mixed = gather([place], [back])
     mixed = lax.switch(
-        over[0], [lambda: rounds(1), lambda: rounds(2), lambda: rounds(-(-SLOTS // cap))]
+        over[0], [lambda: mixed, lambda: rounds(2), lambda: rounds(-(-SLOTS // cap))]
     )
     return call(finish_kernel, shape(1, TP * WIDE), [VMEM])(over_plane(mixed))
 

time: 96.1 us -> 92.4 us (0.961)
  local copies, waits for them, and re-layouts: 2.09 us -> 0.01 us
  Pallas kernels: 7.72 us -> 6.15 us
    pallas_call x1, Pallas kernels: 4.36 us -> 1.91 us  [attend(): call(functools.partial(attend_kernel, cap), (shape(targets, WIDE), jax.Sh...]
    unnamed x6 -> x2, local copies, waits for them, and re-layouts: 2.09 us -> 0.01 us
where the time goes in v3:
time: 92.4 us; the launch traced here: 92.1 us
  blocking collectives  85 us (92%)
  Pallas kernels  6.15 us (7%)
    all_to_all x2, blocking collectives, along_z(): x = lax.all_to_all(x.reshape(nz, -1, WIDE), 'z', 0, 0, tiled=True)  50.4 us
    all_to_all x2, blocking collectives, over_plane(): return lax.all_to_all(x, ('y', 'x', 'c'), 0, 0, tiled=True)  34.6 us
    pallas_call x1, Pallas kernels, attend(): call(functools.partial(attend_kernel, cap), (shape(targets, WIDE), jax.Sh...  1.91 us

profile of v3, /device:TPU:1, one launch (start us, length us, event | category | flops | bytes accessed | tf_op | source)
XLA Modules:
  0.0 92.1 jit_solution(8873448316005793914)
XLA Ops:
  0.0 1.6 %shard_map.46 = bf16[32,16,128]{2,1,0:T(8,128)(2,1)} custom-call(bf16[1,8192]{1,0:T(2,128)(2,1)} %q_hbm.1, s32[4,8]{1,0:T(4,128)} %bitcast.43, s32[8]{0:T(128)} %len_hbm.1), custom_call_target="tpu_custom_call" | custom-call | tf_op jit(solution)/shard_map/pallas_call | solution.py:305
  1.6 18.1 %all_to_all.61.a_ref = bf16[32,16,128]{2,1,0:T(8,128)(2,1)S(1)} all-to-all(bf16[32,16,128]{2,1,0:T(8,128)(2,1)} %shard_map.46), channel_id=1, replica_groups=mesh['z'=16,'y'=4,'x'=4,'c'=2] {'y','x','c'}, dimensions={0} | all-to-all | bytes 262144 | tf_op jit(solution)/shard_map/all_to_all | solution.py:259
  19.7 0.0 copy-start
  19.7 0.8 shard_map.47
  20.5 26.8 %all_to_all.62 = bf16[16,8,1024]{2,1,0:T(8,128)(2,1)S(1)} all-to-all(bf16[16,8,1024]{2,1,0:T(8,128)(2,1)S(1)} %bitcast.37), channel_id=1, replica_groups=mesh['z'=16,'y'=4,'x'=4,'c'=2] {'z'}, dimensions={0} | all-to-all | bytes 524288 | tf_op jit(solution)/shard_map/all_to_all | solution.py:262
  47.3 0.0 copy-done
  47.3 1.9 %shard_map.48 = (bf16[128,1024]{1,0:T(8,128)(2,1)S(1)}, s32[1]{0:T(128)}) custom-call(bf16[128,1024]{1,0:T(8,128)(2,1)S(1)} %bitcast.34, bf16[2,32,256,128]{3,2,1,0:T(8,128)(2,1)S(1)} %copy-done), custom_call_target="tpu_custom_call" | custom-call | tf_op jit(solution)/shard_map/pallas_call | solution.py:275
  49.2 23.6 %all_to_all.63 = bf16[16,8,1024]{2,1,0:T(8,128)(2,1)S(1)} all-to-all(bf16[16,8,1024]{2,1,0:T(8,128)(2,1)S(1)} %bitcast.36), channel_id=1, replica_groups=mesh['z'=16,'y'=4,'x'=4,'c'=2] {'z'}, dimensions={0} | all-to-all | bytes 524288 | tf_op jit(solution)/shard_map/all_to_all | solution.py:262
  72.8 1.1 %shard_map.49 = bf16[32,16,128]{2,1,0:T(8,128)(2,1)S(1)} custom-call(bf16[128,128]{1,0:T(8,128)(2,1)S(1)} %get-tuple-element.71.map_ref, bf16[128,1024]{1,0:T(8,128)(2,1)S(1)} %bitcast.39), custom_call_target="tpu_custom_call" | custom-call | tf_op jit(solution)/shard_map/pallas_call | solution.py:290
  74.6 0.2 conditional.1
  74.8 16.5 %all_to_all.64.d_ref = bf16[32,16,128]{2,1,0:T(8,128)(2,1)S(1)} all-to-all(bf16[32,16,128]{2,1,0:T(8,128)(2,1)S(1)} %get-tuple-element.75), channel_id=1, replica_groups=mesh['z'=16,'y'=4,'x'=4,'c'=2] {'y','x','c'}, dimensions={0} | all-to-all | bytes 262144 | tf_op jit(solution)/shard_map/all_to_all | solution.py:259
  91.3 0.8 shard_map.50
Async XLA Ops:
  19.7 27.6 %copy-start = (bf16[2,32,256,128]{3,2,1,0:T(8,128)(2,1)S(1)}, bf16[2,32,256,128]{3,2,1,0:T(8,128)(2,1)}, u32[]{:S(2)}) copy-start(bf16[2,32,256,128]{3,2,1,0:T(8,128)(2,1)} %kv_ref) | copy-start | bytes 12582916

commit v4 on v3

--- a/solution.py
+++ b/solution.py
@@ -274,7 +274,7 @@
     def attend(got):
         return call(
             functools.partial(attend_kernel, cap),
-            (shape(targets, WIDE), jax.ShapeDtypeStruct((1,), jnp.int32)),
+            (shape(targets, WIDE), pltpu.SMEM((1,), jnp.int32)),
             [VMEM, VMEM],
             [
                 pltpu.VMEM((SLOTS * GROUP, HD), F32),
@@ -312,8 +312,7 @@
             pltpu.SMEM((TP,), jnp.int32),
             pltpu.SemaphoreType.DMA((3,)),
         ],
-        limit=60 << 20,
-    )(queries, block_table.T, lengths)
+    )(*(pltpu.with_memory_space_constraint(x, pltpu.HBM) for x in (queries, block_table.T, lengths)))
     rows = over_plane(fanned)
     out, place = pack(rows, 0)
     got = along_z(out)

time: 92.4 us -> 90.5 us (0.979)
  Pallas kernels: 6.15 us -> 5.09 us
where the time goes in v4:
time: 90.5 us; the launch traced here: 90.2 us
  blocking collectives  84.8 us (94%)
  Pallas kernels  5.09 us (6%)
    all_to_all x2, blocking collectives, along_z(): x = lax.all_to_all(x.reshape(nz, -1, WIDE), 'z', 0, 0, tiled=True)  50.9 us
    all_to_all x2, blocking collectives, over_plane(): return lax.all_to_all(x, ('y', 'x', 'c'), 0, 0, tiled=True)  34 us

profile of v4, /device:TPU:1, one launch (start us, length us, event | category | flops | bytes accessed | tf_op | source)
XLA Modules:
  0.0 90.2 jit_solution(8964886214637655732)
XLA Ops:
  0.0 0.9 %shard_map.46 = bf16[32,16,128]{2,1,0:T(8,128)(2,1)S(1)} custom-call(bf16[1,8192]{1,0:T(2,128)(2,1)} %q_hbm.1, s32[4,8]{1,0:T(4,128)} %bitcast.43, s32[8]{0:T(128)} %len_hbm.1), custom_call_target="tpu_custom_call" | custom-call | tf_op jit(solution)/shard_map/pallas_call | solution.py:305
  0.9 17.2 %all_to_all.61.a_ref = bf16[32,16,128]{2,1,0:T(8,128)(2,1)S(1)} all-to-all(bf16[32,16,128]{2,1,0:T(8,128)(2,1)S(1)} %shard_map.46), channel_id=1, replica_groups=mesh['z'=16,'y'=4,'x'=4,'c'=2] {'y','x','c'}, dimensions={0} | all-to-all | bytes 262144 | tf_op jit(solution)/shard_map/all_to_all | solution.py:259
  18.2 0.0 copy-start
  18.2 0.8 shard_map.47
  19.0 27.5 %all_to_all.62 = bf16[16,8,1024]{2,1,0:T(8,128)(2,1)S(1)} all-to-all(bf16[16,8,1024]{2,1,0:T(8,128)(2,1)S(1)} %bitcast.37), channel_id=1, replica_groups=mesh['z'=16,'y'=4,'x'=4,'c'=2] {'z'}, dimensions={0} | all-to-all | bytes 524288 | tf_op jit(solution)/shard_map/all_to_all | solution.py:262
  46.5 0.0 copy-done
  46.5 1.5 %shard_map.48 = (bf16[128,1024]{1,0:T(8,128)(2,1)S(1)}, s32[1]{0:T(128)S(4)}) custom-call(bf16[128,1024]{1,0:T(8,128)(2,1)S(1)} %bitcast.34, bf16[2,32,256,128]{3,2,1,0:T(8,128)(2,1)S(1)} %copy-done), custom_call_target="tpu_custom_call" | custom-call | tf_op jit(solution)/shard_map/pallas_call | solution.py:275
  47.9 23.4 %all_to_all.63 = bf16[16,8,1024]{2,1,0:T(8,128)(2,1)S(1)} all-to-all(bf16[16,8,1024]{2,1,0:T(8,128)(2,1)S(1)} %bitcast.36), channel_id=1, replica_groups=mesh['z'=16,'y'=4,'x'=4,'c'=2] {'z'}, dimensions={0} | all-to-all | bytes 524288 | tf_op jit(solution)/shard_map/all_to_all | solution.py:262
  71.3 1.1 %shard_map.49 = bf16[32,16,128]{2,1,0:T(8,128)(2,1)S(1)} custom-call(bf16[128,128]{1,0:T(8,128)(2,1)S(1)} %get-tuple-element.71.map_ref, bf16[128,1024]{1,0:T(8,128)(2,1)S(1)} %bitcast.39), custom_call_target="tpu_custom_call" | custom-call | tf_op jit(solution)/shard_map/pallas_call | solution.py:290
  72.5 0.2 conditional.1
  72.7 16.7 %all_to_all.64.d_ref = bf16[32,16,128]{2,1,0:T(8,128)(2,1)S(1)} all-to-all(bf16[32,16,128]{2,1,0:T(8,128)(2,1)S(1)} %get-tuple-element.75), channel_id=1, replica_groups=mesh['z'=16,'y'=4,'x'=4,'c'=2] {'y','x','c'}, dimensions={0} | all-to-all | bytes 262144 | tf_op jit(solution)/shard_map/all_to_all | solution.py:259
  89.4 0.8 shard_map.50
Async XLA Ops:
  18.2 28.3 %copy-start = (bf16[2,32,256,128]{3,2,1,0:T(8,128)(2,1)S(1)}, bf16[2,32,256,128]{3,2,1,0:T(8,128)(2,1)}, u32[]{:S(2)}) copy-start(bf16[2,32,256,128]{3,2,1,0:T(8,128)(2,1)} %kv_ref) | copy-start | bytes 12582916

commit v5 on v4

--- a/solution.py
+++ b/solution.py
@@ -34,6 +34,10 @@
 
 def lanes(shape):
     return lax.broadcasted_iota(jnp.int32, shape, len(shape) - 1)
+
+
+def up(shape):
+    return lax.broadcasted_iota(jnp.int32, shape, 0)
 
 
 def fan_kernel(q_hbm, table_hbm, len_hbm, out_ref, q_ref, table_ref, len_ref, sems):
@@ -72,37 +76,37 @@
         [scr[pl.ds(g, ROWS, stride=16), :] for g in range(GROUP)], axis=1
     ).astype(BF16)
     extra = scr[pl.ds(GROUP, ROWS, stride=16), :]
-    pool = jnp.concatenate([extra[:, b : b + 1] for b in range(MAXB)], axis=0)
-    slot = jnp.concatenate([extra[:, MAXB + b : MAXB + b + 1] for b in range(MAXB)], axis=0)
-    length = extra[:, 8:9] * SLOTS + extra[:, 9:10]
-    filled = jnp.concatenate([length - b * BLK for b in range(MAXB)], axis=0)
+    extra = extra.T
+    pool = jnp.concatenate([extra[b : b + 1] for b in range(MAXB)], axis=1)
+    slot = jnp.concatenate([extra[MAXB + b : MAXB + b + 1] for b in range(MAXB)], axis=1)
+    length = extra[8:9] * SLOTS + extra[9:10]
+    filled = jnp.concatenate([length - b * BLK for b in range(MAXB)], axis=1)
     filled = jnp.clip(filled, 0.0, float(BLK))
     dest = jnp.floor(pool * (1.0 / NY))
     valid = (pool - dest * NY == y) & (filled > 0.0)
     entries = MAXB * ROWS
-    lane = lanes((entries, HD))
-    member = jnp.where((lane.astype(F32) == dest) & valid, 1.0, 0.0)
-    earlier = jnp.where(
-        lax.broadcasted_iota(jnp.int32, (entries, entries), 0) > lanes((entries, entries)), 1.0, 0.0
-    ).astype(BF16)
-    before = dot(earlier, member.astype(BF16), ((1,), (0,)))
-    rank = jnp.sum(before * member, axis=1, keepdims=True)
-    most = jnp.max(jnp.sum(member, axis=0, keepdims=True))
+    planes = targets // tall
+    member = jnp.where((up((planes, entries)).astype(F32) == dest) & valid, 1.0, 0.0)
+    earlier = jnp.where(up((entries, entries)) < lanes((entries, entries)), 1.0, 0.0)
+    before = dot(member.astype(BF16), earlier.astype(BF16), ((1,), (0,)))
+    rank = jnp.sum(before * member, axis=0, keepdims=True)
+    most = jnp.max(jnp.sum(member, axis=1, keepdims=True), axis=0, keepdims=True)
     rank = rank - skip
     fits = valid & (rank >= 0.0) & (rank < cap)
-    column = lanes((entries, targets)).astype(F32)
-    place = jnp.where(column == jnp.where(fits, dest * tall + rank, -1.0), 1.0, 0.0).astype(BF16)
-    last = jnp.where(column == jnp.where(fits, dest * tall + cap, -1.0), 1.0, 0.0).astype(BF16)
-    map_ref[...] = place
-    mine = jnp.where(lane % 2 == 0, slot + 1.0, filled)
-    mine = jnp.where((lane // 2).astype(F32) == rank, mine, 0.0).astype(BF16)
+    spot = up((targets, entries)).astype(F32)
+    place = jnp.where(spot == jnp.where(fits, dest * tall + rank, -1.0), 1.0, 0.0)
+    last = jnp.where(spot == jnp.where(fits, dest * tall + cap, -1.0), 1.0, 0.0).astype(BF16)
+    side = up((HD, entries))
+    mine = jnp.where(side % 2 == 0, slot + 1.0, filled)
+    mine = jnp.where((side // 2).astype(F32) == rank, mine, 0.0).astype(BF16)
     four = jnp.concatenate([query] * MAXB, axis=0)
-    out_ref[...] = dot(place, four, ((0,), (0,))).astype(BF16)
-    numbers = dot(last, mine, ((0,), (0,)))
+    out = dot(place.astype(BF16), four, ((1,), (0,)))
+    out_ref[:, HD:] = out[:, HD:].astype(BF16)
+    numbers = dot(last, mine, ((1,), (1,)))
     numbers = jnp.where(lanes((targets, HD)) == 2 * cap, most, numbers)
-    final = lax.broadcasted_iota(jnp.int32, (targets, HD), 0) % tall == cap
-    head = out_ref[:, :HD].astype(F32)
-    out_ref[:, :HD] = jnp.where(final, numbers, head).astype(BF16)
+    final = up((targets, HD)) % tall == cap
+    out_ref[:, :HD] = jnp.where(final, numbers, out[:, :HD]).astype(BF16)
+    map_ref[...] = place.T.astype(BF16)
 
 
 def own_lanes(x, tall, width):
@@ -124,13 +128,14 @@
         jnp.where((row % tall == cap) & (lane == 2 * cap), numbers.astype(F32), 0.0)
     )
     most_ref[0] = jnp.where(most > 2 * cap, 2, jnp.where(most > cap, 1, 0))
-    own = own_lanes(numbers, tall, 2)
-    slot = jnp.sum(jnp.where(lane % 2 == 0, own, 0.0), axis=1, keepdims=True) - 1.0
-    filled = jnp.sum(jnp.where(lane % 2 == 1, own, 0.0), axis=1, keepdims=True)
-    place = jnp.where(lanes((targets, SLOTS)).astype(F32) == slot, 1.0, 0.0).astype(BF16)
-    got = dot(place, b_ref[...], ((0,), (0,)))
-    filled = jnp.broadcast_to(filled, (targets, HD)).astype(BF16)
-    filled = dot(place, filled, ((0,), (0,)))
+    own = own_lanes(numbers, tall, 2).astype(BF16)
+    odd = jnp.where(lanes((8, HD)) % 2 == up((8, HD)), 1.0, 0.0).astype(BF16)
+    pair = dot(odd, own, ((1,), (1,)))
+    place = jnp.where(up((SLOTS, targets)).astype(F32) == pair[0:1] - 1.0, 1.0, 0.0)
+    filled = jnp.sum(place * pair[1:2], axis=1, keepdims=True)
+    filled = jnp.broadcast_to(filled, (SLOTS, HD))
+    back_place = place.T.astype(BF16)
+    got = dot(place.astype(BF16), b_ref[...], ((1,), (0,)))
     for g in range(GROUP):
         rows = pl.ds(g, SLOTS, stride=GROUP)
         q_scr[rows, :] = got[:, g * HD : (g + 1) * HD]
@@ -164,16 +169,16 @@
         coarse = jnp.where(lane == 2 * g, hi, jnp.where(lane == 2 * g + 1, mid, coarse))
         fine = jnp.where(lane == 2 * g, lo, fine)
     back = jnp.concatenate(parts, axis=1).astype(BF16)
-    out_ref[...] = dot(place, back, ((1,), (0,))).astype(BF16)
+    out = dot(back_place, back, ((1,), (0,)))
+    out_ref[:, 2 * HD :] = out[:, 2 * HD :].astype(BF16)
     final = row % tall == cap
     lane = lanes((targets, HD))
     for k, part in enumerate((coarse, fine)):
-        each = dot(place, part.astype(BF16), ((1,), (0,)))
+        each = dot(back_place, part.astype(BF16), ((1,), (0,)))
         each = jnp.where(lane // 16 == row % tall, each, 0.0).reshape(targets // tall, tall, HD)
         both = jnp.broadcast_to(jnp.sum(each, axis=1, keepdims=True), each.shape)
         spot = slice(k * HD, (k + 1) * HD)
-        head = out_ref[:, spot].astype(F32)
-        out_ref[:, spot] = jnp.where(final, both.reshape(targets, HD), head).astype(BF16)
+        out_ref[:, spot] = jnp.where(final, both.reshape(targets, HD), out[:, spot]).astype(BF16)
 
 
 def gather_kernel(cap, map_ref, c_ref, out_ref, scr):
@@ -182,20 +187,20 @@
     fine = own_lanes(c_ref[:, HD : 2 * HD], tall, 16).astype(BF16)
     pick = lax.broadcasted_iota(jnp.int32, (HD, HD), 0) % 16 // 2 == lanes((HD, HD))
     pick = jnp.where(pick, 1.0, 0.0).astype(BF16)
-    got, ok, levels = [], [], []
-    for b in range(MAXB):
-        place = map_ref[b * ROWS : (b + 1) * ROWS, :]
-        got.append(dot(place, c_ref[...], ((1,), (0,))))
-        ok.append(jnp.sum(place.astype(F32), axis=1, keepdims=True) > 0.0)
-        level = 0.0
-        for part in (coarse, fine):
-            part = dot(place, part, ((1,), (0,))).astype(BF16)
-            level = level + dot(part, pick, ((1,), (0,)))
-        levels.append(level)
+    place = map_ref[...]
+    got = dot(place, c_ref[...], ((1,), (0,)))
+    level = 0.0
+    for part in (coarse, fine):
+        part = dot(place, part, ((1,), (0,))).astype(BF16)
+        level = level + dot(part, pick, ((1,), (0,)))
+    found = jnp.sum(place.astype(F32), axis=1, keepdims=True) > 0.0
+    level = jnp.where(found, level, NEG)
+    blocks = [slice(b * ROWS, (b + 1) * ROWS) for b in range(MAXB)]
+    levels = [level[b] for b in blocks]
+    ok = [found[b] for b in blocks]
+    got = [got[b] for b in blocks]
     lane = lanes((ROWS, HD))
-    top = functools.reduce(
-        jnp.maximum, [jnp.where(o, level, NEG) for o, level in zip(ok, levels)]
-    )
+    top = functools.reduce(jnp.maximum, levels)
     factor = [jnp.where(o, jnp.exp(level - top), 0.0) for o, level in zip(ok, levels)]
     total = functools.reduce(jnp.add, factor)
     any_ok = total > 0.0

time: 90.5 us -> 89.6 us (0.990)
  no operation moved by 1% of the time
where the time goes in v5:
time: 89.6 us; the launch traced here: 89.3 us
  blocking collectives  84.8 us (95%)
  Pallas kernels  4.44 us (5%)
    all_to_all x2, blocking collectives, along_z(): x = lax.all_to_all(x.reshape(nz, -1, WIDE), 'z', 0, 0, tiled=True)  50.9 us
    all_to_all x2, blocking collectives, over_plane(): return lax.all_to_all(x, ('y', 'x', 'c'), 0, 0, tiled=True)  34 us

profile of v5, /device:TPU:1, one launch (start us, length us, event | category | flops | bytes accessed | tf_op | source)
XLA Modules:
  0.0 89.3 jit_solution(17103690396894245851)
XLA Ops:
  0.0 0.9 %shard_map.46 = bf16[32,16,128]{2,1,0:T(8,128)(2,1)S(1)} custom-call(bf16[1,8192]{1,0:T(2,128)(2,1)} %q_hbm.1, s32[4,8]{1,0:T(4,128)} %bitcast.43, s32[8]{0:T(128)} %len_hbm.1), custom_call_target="tpu_custom_call" | custom-call | tf_op jit(solution)/shard_map/pallas_call | solution.py:310
  0.9 17.2 %all_to_all.61.a_ref = bf16[32,16,128]{2,1,0:T(8,128)(2,1)S(1)} all-to-all(bf16[32,16,128]{2,1,0:T(8,128)(2,1)S(1)} %shard_map.46), channel_id=1, replica_groups=mesh['z'=16,'y'=4,'x'=4,'c'=2] {'y','x','c'}, dimensions={0} | all-to-all | bytes 262144 | tf_op jit(solution)/shard_map/all_to_all | solution.py:264
  18.2 0.0 copy-start
  18.2 0.5 shard_map.47
  18.7 27.5 %all_to_all.62 = bf16[16,8,1024]{2,1,0:T(8,128)(2,1)S(1)} all-to-all(bf16[16,8,1024]{2,1,0:T(8,128)(2,1)S(1)} %bitcast.37), channel_id=1, replica_groups=mesh['z'=16,'y'=4,'x'=4,'c'=2] {'z'}, dimensions={0} | all-to-all | bytes 524288 | tf_op jit(solution)/shard_map/all_to_all | solution.py:267
  46.2 0.0 copy-done
  46.2 1.5 %shard_map.48 = (bf16[128,1024]{1,0:T(8,128)(2,1)S(1)}, s32[1]{0:T(128)S(4)}) custom-call(bf16[128,1024]{1,0:T(8,128)(2,1)S(1)} %bitcast.34, bf16[2,32,256,128]{3,2,1,0:T(8,128)(2,1)S(1)} %copy-done), custom_call_target="tpu_custom_call" | custom-call | tf_op jit(solution)/shard_map/pallas_call | solution.py:280
  47.7 23.4 %all_to_all.63 = bf16[16,8,1024]{2,1,0:T(8,128)(2,1)S(1)} all-to-all(bf16[16,8,1024]{2,1,0:T(8,128)(2,1)S(1)} %bitcast.36), channel_id=1, replica_groups=mesh['z'=16,'y'=4,'x'=4,'c'=2] {'z'}, dimensions={0} | all-to-all | bytes 524288 | tf_op jit(solution)/shard_map/all_to_all | solution.py:267
  71.0 0.8 shard_map.49
  71.8 16.7 %all_to_all.64.d_ref = bf16[32,16,128]{2,1,0:T(8,128)(2,1)S(1)} all-to-all(bf16[32,16,128]{2,1,0:T(8,128)(2,1)S(1)} %get-tuple-element.75), channel_id=1, replica_groups=mesh['z'=16,'y'=4,'x'=4,'c'=2] {'y','x','c'}, dimensions={0} | all-to-all | bytes 262144 | tf_op jit(solution)/shard_map/all_to_all | solution.py:264
  88.5 0.8 shard_map.50
  (1 shorter events, 0.0 us)
Async XLA Ops:
  18.2 28.0 %copy-start = (bf16[2,32,256,128]{3,2,1,0:T(8,128)(2,1)S(1)}, bf16[2,32,256,128]{3,2,1,0:T(8,128)(2,1)}, u32[]{:S(2)}) copy-start(bf16[2,32,256,128]{3,2,1,0:T(8,128)(2,1)} %kv_ref) | copy-start | bytes 12582916

commit v6 on v5

--- a/solution.py
+++ b/solution.py
@@ -17,6 +17,7 @@
 SLOTS = 32
 ROWS = NY * TP
 WIDE = GROUP * HD
+HALF = TP * GROUP // 2
 NEG = -1e30
 F32 = jnp.float32
 BF16 = jnp.bfloat16
@@ -62,6 +63,7 @@
     extra = jnp.where(lane == 9, (length % SLOTS).astype(F32), extra)
     q = q_ref[...].astype(F32)
     heads = jnp.concatenate([q[:, h * HD : (h + 1) * HD] for h in range(TP * GROUP)], axis=0)
+    heads = jnp.concatenate([heads[HALF:], heads[:HALF]], axis=0)
     both = jnp.concatenate([heads.reshape(TP, GROUP, HD), extra], axis=1).astype(BF16)
     for y in range(NY):
         out_ref[y * TP : (y + 1) * TP] = both
@@ -86,6 +88,7 @@
     valid = (pool - dest * NY == y) & (filled > 0.0)
     entries = MAXB * ROWS
     planes = targets // tall
+    dest = jnp.where(dest < planes // 2, dest + planes // 2, dest - planes // 2)
     member = jnp.where((up((planes, entries)).astype(F32) == dest) & valid, 1.0, 0.0)
     earlier = jnp.where(up((entries, entries)) < lanes((entries, entries)), 1.0, 0.0)
     before = dot(member.astype(BF16), earlier.astype(BF16), ((1,), (0,)))
@@ -231,6 +234,7 @@
     total = functools.reduce(jnp.add, factor)
     mixed = functools.reduce(jnp.add, [f * p for f, p in zip(factor, parts)])
     result = (mixed / total).reshape(TP * GROUP, HD)
+    result = jnp.concatenate([result[HALF:], result[:HALF]], axis=0)
     out_ref[...] = jnp.concatenate(
         [result[h : h + 1, :] for h in range(TP * GROUP)], axis=1
     ).astype(BF16)
@@ -261,10 +265,18 @@
     targets = nz * (cap + 1)
 
     def over_plane(x):
-        return lax.all_to_all(x, ("y", "x", "c"), 0, 0, tiled=True)
+        turned = [
+            ((y + NY // 2) % NY) * TP + (t + TP // 2) % TP for y in range(NY) for t in range(TP)
+        ]
+        return lax.all_to_all(
+            x, ("y", "x", "c"), 0, 0, tiled=True, axis_index_groups=[turned]
+        )
 
     def along_z(x):
-        x = lax.all_to_all(x.reshape(nz, -1, WIDE), "z", 0, 0, tiled=True)
+        turned = [[(k + nz // 2) % nz for k in range(nz)]]
+        x = lax.all_to_all(
+            x.reshape(nz, -1, WIDE), "z", 0, 0, tiled=True, axis_index_groups=turned
+        )
         return x.reshape(-1, WIDE)
 
     def pack(rows, skip):

time: 89.6 us -> 83.6 us (0.933)
  blocking collectives: 84.8 us -> 78.8 us
    all_to_all x4, blocking collectives: 84.8 us -> 78.8 us  [the longest x2 50.7 us: along_z(): lax.all_to_all(x.reshape(nz, -1, WIDE), 'z', 0, 0, tiled=True, axis_index...]
where the time goes in v6:
time: 83.6 us; the launch traced here: 83.3 us
  blocking collectives  78.8 us (94%)
  Pallas kernels  4.42 us (5%)
    all_to_all x2, blocking collectives, along_z(): lax.all_to_all(x.reshape(nz, -1, WIDE), 'z', 0, 0, tiled=True, axis_index...  50.7 us
    all_to_all x2, blocking collectives, over_plane(): lax.all_to_all(x, ('y', 'x', 'c'), 0, 0, tiled=True, axis_index_groups=[t...  28.1 us

profile of v6, /device:TPU:1, one launch (start us, length us, event | category | flops | bytes accessed | tf_op | source)
XLA Modules:
  0.0 83.3 jit_solution(2666979847466067867)
XLA Ops:
  0.0 0.9 %shard_map.46 = bf16[32,16,128]{2,1,0:T(8,128)(2,1)S(1)} custom-call(bf16[1,8192]{1,0:T(2,128)(2,1)} %q_hbm.1, s32[4,8]{1,0:T(4,128)} %bitcast.43, s32[8]{0:T(128)} %len_hbm.1), custom_call_target="tpu_custom_call" | custom-call | tf_op jit(solution)/shard_map/pallas_call | solution.py:322
  0.9 16.5 %all_to_all.61.a_ref = bf16[32,16,128]{2,1,0:T(8,128)(2,1)S(1)} all-to-all(bf16[32,16,128]{2,1,0:T(8,128)(2,1)S(1)} %shard_map.46), channel_id=1, replica_groups={{20,21,22,23,16,17,18,19,28,29,30,31,24,25,26,27,4,5,6,7,0,1,2,3,12,13,..., dimensions={0} | all-to-all | bytes 262144 | tf_op jit(solution)/shard_map/all_to_all | solution.py:271
  17.4 0.0 copy-start
  17.4 0.5 shard_map.47
  17.9 27.2 %all_to_all.62 = bf16[16,8,1024]{2,1,0:T(8,128)(2,1)S(1)} all-to-all(bf16[16,8,1024]{2,1,0:T(8,128)(2,1)S(1)} %bitcast.37), channel_id=1, replica_groups={{256,288,320,352,384,416,448,480,0,32,64,96,128,160,192,224},{257,289,3..., dimensions={0} | all-to-all | bytes 524288 | tf_op jit(solution)/shard_map/all_to_all | solution.py:277
  45.1 0.0 copy-done
  45.1 1.5 %shard_map.48 = (bf16[128,1024]{1,0:T(8,128)(2,1)S(1)}, s32[1]{0:T(128)S(4)}) custom-call(bf16[128,1024]{1,0:T(8,128)(2,1)S(1)} %bitcast.34, bf16[2,32,256,128]{3,2,1,0:T(8,128)(2,1)S(1)} %copy-done), custom_call_target="tpu_custom_call" | custom-call | tf_op jit(solution)/shard_map/pallas_call | solution.py:292
  46.6 23.5 %all_to_all.63 = bf16[16,8,1024]{2,1,0:T(8,128)(2,1)S(1)} all-to-all(bf16[16,8,1024]{2,1,0:T(8,128)(2,1)S(1)} %bitcast.36), channel_id=1, replica_groups={{256,288,320,352,384,416,448,480,0,32,64,96,128,160,192,224},{257,289,3..., dimensions={0} | all-to-all | bytes 524288 | tf_op jit(solution)/shard_map/all_to_all | solution.py:277
  70.1 0.8 shard_map.49
  70.9 11.6 %all_to_all.64.d_ref = bf16[32,16,128]{2,1,0:T(8,128)(2,1)S(1)} all-to-all(bf16[32,16,128]{2,1,0:T(8,128)(2,1)S(1)} %get-tuple-element.75), channel_id=1, replica_groups={{20,21,22,23,16,17,18,19,28,29,30,31,24,25,26,27,4,5,6,7,0,1,2,3,12,13,..., dimensions={0} | all-to-all | bytes 262144 | tf_op jit(solution)/shard_map/all_to_all | solution.py:271
  82.5 0.8 shard_map.50
  (1 shorter events, 0.0 us)
Async XLA Ops:
  17.4 27.7 %copy-start = (bf16[2,32,256,128]{3,2,1,0:T(8,128)(2,1)S(1)}, bf16[2,32,256,128]{3,2,1,0:T(8,128)(2,1)}, u32[]{:S(2)}) copy-start(bf16[2,32,256,128]{3,2,1,0:T(8,128)(2,1)} %kv_ref) | copy-start | bytes 12582916

commit v7 on v5

--- a/solution.py
+++ b/solution.py
@@ -10,13 +10,17 @@
 
 HD = 128
 NY = 4
+FAR = 4
 TP = 8
 GROUP = 8
 MAXB = 4
 BLK = 256
 SLOTS = 32
-ROWS = NY * TP
+ROWS = FAR * TP
 WIDE = GROUP * HD
+HALF = WIDE // 2
+LONG = HALF + HD
+SPAN = GROUP // 2
 NEG = -1e30
 F32 = jnp.float32
 BF16 = jnp.bfloat16
@@ -38,6 +42,10 @@
 
 def up(shape):
     return lax.broadcasted_iota(jnp.int32, shape, 0)
+
+
+def opposite(place, size):
+    return jnp.where(place < size // 2, place + size // 2, place - size // 2)
 
 
 def fan_kernel(q_hbm, table_hbm, len_hbm, out_ref, q_ref, table_ref, len_ref, sems):
@@ -51,8 +59,8 @@
     for copy in copies:
         copy.wait()
     t = lax.axis_index("x") * 2 + lax.axis_index("c")
-    lane = lanes((TP, GROUP, HD))
-    extra = jnp.zeros((TP, GROUP, HD), F32)
+    lane = lanes((2 * TP, HD))
+    extra = jnp.zeros((2 * TP, HD), F32)
     for b in range(MAXB):
         slot = table_ref[b, t]
         extra = jnp.where(lane == b, (slot // SLOTS).astype(F32), extra)
@@ -61,31 +69,37 @@
     extra = jnp.where(lane == 8, (length // SLOTS).astype(F32), extra)
     extra = jnp.where(lane == 9, (length % SLOTS).astype(F32), extra)
     q = q_ref[...].astype(F32)
-    heads = jnp.concatenate([q[:, h * HD : (h + 1) * HD] for h in range(TP * GROUP)], axis=0)
-    both = jnp.concatenate([heads.reshape(TP, GROUP, HD), extra], axis=1).astype(BF16)
-    for y in range(NY):
-        out_ref[y * TP : (y + 1) * TP] = both
+    halves = [q[:, i * HALF : (i + 1) * HALF] for i in range(2 * TP)]
+    heads = jnp.concatenate(halves[TP:] + halves[:TP], axis=0)
+    both = jnp.concatenate([heads, extra], axis=1).reshape(TP, 2, LONG).astype(BF16)
+    for far in range(FAR):
+        out_ref[far * TP : (far + 1) * TP] = both
 
 
 def pack_kernel(cap, skip, a_ref, kv_hbm, out_ref, map_ref, scr):
-    y = lax.axis_index("y").astype(F32)
+    quarter = lax.axis_index("zh").astype(F32)
     targets = out_ref.shape[0]
     tall = cap + 1
-    scr[...] = a_ref[...].reshape(ROWS * 16, HD).astype(F32)
+    both = a_ref[...].astype(F32).reshape(ROWS * 2, LONG)
+    for k in range(SPAN + 1):
+        scr[k] = both[:, k * HD : (k + 1) * HD]
     query = jnp.concatenate(
-        [scr[pl.ds(g, ROWS, stride=16), :] for g in range(GROUP)], axis=1
+        [scr[k, pl.ds(half, ROWS, stride=2), :] for half in range(2) for k in range(SPAN)], axis=1
     ).astype(BF16)
-    extra = scr[pl.ds(GROUP, ROWS, stride=16), :]
-    extra = extra.T
+    extra = scr[SPAN, pl.ds(0, ROWS, stride=2), :].T
     pool = jnp.concatenate([extra[b : b + 1] for b in range(MAXB)], axis=1)
     slot = jnp.concatenate([extra[MAXB + b : MAXB + b + 1] for b in range(MAXB)], axis=1)
     length = extra[8:9] * SLOTS + extra[9:10]
     filled = jnp.concatenate([length - b * BLK for b in range(MAXB)], axis=1)
     filled = jnp.clip(filled, 0.0, float(BLK))
-    dest = jnp.floor(pool * (1.0 / NY))
-    valid = (pool - dest * NY == y) & (filled > 0.0)
+    planes = targets // tall
+    holder = jnp.floor(pool * (1.0 / planes))
+    dest = pool - holder * planes
+    plane = jnp.floor(dest * (1.0 / NY))
+    column = opposite(dest - plane * NY, NY)
+    dest = opposite(plane, planes // NY) * NY + column
+    valid = (holder == quarter) & (filled > 0.0)
     entries = MAXB * ROWS
-    planes = targets // tall
     member = jnp.where((up((planes, entries)).astype(F32) == dest) & valid, 1.0, 0.0)
     earlier = jnp.where(up((entries, entries)) < lanes((entries, entries)), 1.0, 0.0)
     before = dot(member.astype(BF16), earlier.astype(BF16), ((1,), (0,)))
@@ -185,7 +199,7 @@
     tall = cap + 1
     coarse = own_lanes(c_ref[:, :HD], tall, 16).astype(BF16)
     fine = own_lanes(c_ref[:, HD : 2 * HD], tall, 16).astype(BF16)
-    pick = lax.broadcasted_iota(jnp.int32, (HD, HD), 0) % 16 // 2 == lanes((HD, HD))
+    pick = up((HD, HD)) % 16 // 2 == lanes((HD, HD)) % GROUP
     pick = jnp.where(pick, 1.0, 0.0).astype(BF16)
     place = map_ref[...]
     got = dot(place, c_ref[...], ((1,), (0,)))
@@ -207,33 +221,42 @@
     total = jnp.where(any_ok, total, 1.0)
     three = split(jnp.where(any_ok, top + jnp.log(total), NEG))
     factor = [f / total for f in factor]
-    for g in range(GROUP):
-        mixed = functools.reduce(
-            jnp.add,
-            [factor[b][:, g : g + 1] * got[b][:, g * HD : (g + 1) * HD] for b in range(MAXB)],
-        )
-        scr[pl.ds(g, ROWS, stride=16), :] = mixed
-        hi, mid, lo = [part[:, g : g + 1] for part in three]
-        scr[pl.ds(GROUP + g, ROWS, stride=16), :] = jnp.where(
-            lane == 0, hi, jnp.where(lane == 1, mid, jnp.where(lane == 2, lo, 0.0))
-        )
-    out_ref[...] = scr[...].reshape(ROWS, 16, HD).astype(BF16)
+    extra = jnp.zeros((ROWS, HD), F32)
+    for k, part in enumerate(three):
+        extra = jnp.where(lane // GROUP == k, part, extra)
+    for half in range(2):
+        rows = pl.ds(half, ROWS, stride=2)
+        for k in range(SPAN):
+            g = half * SPAN + k
+            mixed = [factor[b][:, g : g + 1] * got[b][:, g * HD : (g + 1) * HD] for b in range(MAXB)]
+            scr[k, rows, :] = functools.reduce(jnp.add, mixed)
+        scr[SPAN, rows, :] = extra
+    both = jnp.concatenate([scr[k] for k in range(SPAN + 1)], axis=1)
+    out_ref[...] = both.reshape(ROWS, 2, LONG).astype(BF16)
 
 
 def finish_kernel(d_ref, out_ref):
     parts, level = [], []
-    for y in range(NY):
-        x = d_ref[y * TP : (y + 1) * TP].astype(F32)
-        parts.append(x[:, :GROUP, :])
-        level.append(jnp.sum(x[:, GROUP:, :], axis=2, keepdims=True))
-    top = functools.reduce(jnp.maximum, level)
-    factor = [jnp.exp(one - top) for one in level]
-    total = functools.reduce(jnp.add, factor)
-    mixed = functools.reduce(jnp.add, [f * p for f, p in zip(factor, parts)])
-    result = (mixed / total).reshape(TP * GROUP, HD)
-    out_ref[...] = jnp.concatenate(
-        [result[h : h + 1, :] for h in range(TP * GROUP)], axis=1
-    ).astype(BF16)
+    lane = lanes((2 * TP, HD))
+    first = up((2 * TP, HD)) % 2 * SPAN
+    mine = [(lane % GROUP == first + k) & (lane < 3 * GROUP) for k in range(SPAN)]
+    for far in range(FAR):
+        x = d_ref[far * TP : (far + 1) * TP].astype(F32).reshape(2 * TP, LONG)
+        parts.append(x[:, :HALF])
+        numbers = x[:, HALF:]
+        level.append(
+            [jnp.sum(jnp.where(m, numbers, 0.0), axis=1, keepdims=True) for m in mine]
+        )
+    result = []
+    for k in range(SPAN):
+        top = functools.reduce(jnp.maximum, [one[k] for one in level])
+        factor = [jnp.exp(one[k] - top) for one in level]
+        total = functools.reduce(jnp.add, factor)
+        mixed = [f * p[:, k * HD : (k + 1) * HD] for f, p in zip(factor, parts)]
+        result.append(functools.reduce(jnp.add, mixed) / total)
+    result = jnp.concatenate(result, axis=1)
+    halves = [result[i : i + 1] for i in range(2 * TP)]
+    out_ref[...] = jnp.concatenate(halves[TP:] + halves[:TP], axis=1).astype(BF16)
 
 
 SMEM = pl.BlockSpec(memory_space=pltpu.SMEM)
@@ -257,14 +280,22 @@
 
 
 def per_device(cap, queries, kv_pool, block_table, lengths):
-    nz = lax.axis_size("z")
-    targets = nz * (cap + 1)
-
-    def over_plane(x):
-        return lax.all_to_all(x, ("y", "x", "c"), 0, 0, tiled=True)
-
-    def along_z(x):
-        x = lax.all_to_all(x.reshape(nz, -1, WIDE), "z", 0, 0, tiled=True)
+    near = ("zl", "y")
+    pools = lax.axis_size(near)
+    targets = pools * (cap + 1)
+
+    def turned(slow, fast):
+        return [[(i + slow // 2) % slow * fast + (j + fast // 2) % fast for i in range(slow) for j in range(fast)]]
+
+    def over_far(x):
+        return lax.all_to_all(
+            x, ("zh", "x", "c"), 0, 0, tiled=True, axis_index_groups=turned(FAR, TP)
+        )
+
+    def over_near(x):
+        x = x.reshape(pools, -1, WIDE)
+        groups = turned(pools // NY, NY)
+        x = lax.all_to_all(x, near, 0, 0, tiled=True, axis_index_groups=groups)
         return x.reshape(-1, WIDE)
 
     def pack(rows, skip):
@@ -272,7 +303,7 @@
             functools.partial(pack_kernel, cap, skip),
             (shape(targets, WIDE), shape(MAXB * ROWS, targets)),
             [VMEM, HBM],
-            [pltpu.VMEM((ROWS * 16, HD), F32)],
+            [pltpu.VMEM((SPAN + 1, ROWS * 2, HD), F32)],
             (VMEM, VMEM),
         )(rows, kv_pool)
 
@@ -294,9 +325,9 @@
     def gather(places, backs):
         return call(
             functools.partial(gather_kernel, cap),
-            shape(ROWS, 16, HD),
+            shape(ROWS, 2, LONG),
             [VMEM, VMEM],
-            [pltpu.VMEM((ROWS * 16, HD), F32)],
+            [pltpu.VMEM((SPAN + 1, ROWS * 2, HD), F32)],
         )(jnp.concatenate(places, axis=1), jnp.concatenate(backs, axis=0))
 
     def rounds(count):
@@ -304,12 +335,12 @@
         for k in range(1, count):
             out, more = pack(rows, k * cap)
             places.append(more)
-            backs.append(along_z(attend(along_z(out))[0]))
+            backs.append(over_near(attend(over_near(out))[0]))
         return gather(places, backs)
 
     fanned = call(
         fan_kernel,
-        shape(ROWS, 16, HD),
+        shape(ROWS, 2, LONG),
         [HBM, HBM, HBM],
         [
             pltpu.VMEM((1, TP * WIDE), BF16),
@@ -318,31 +349,33 @@
             pltpu.SemaphoreType.DMA((3,)),
         ],
     )(*(pltpu.with_memory_space_constraint(x, pltpu.HBM) for x in (queries, block_table.T, lengths)))
-    rows = over_plane(fanned)
+    rows = over_far(fanned)
     out, place = pack(rows, 0)
-    got = along_z(out)
+    got = over_near(out)
     got, place, rows, kv_pool = lax.optimization_barrier((got, place, rows, kv_pool))
     back, over = attend(got)
-    back = along_z(back)
+    back = over_near(back)
     back, place, rows, over, kv_pool = lax.optimization_barrier((back, place, rows, over, kv_pool))
     mixed = gather([place], [back])
     mixed = lax.switch(
         over[0], [lambda: mixed, lambda: rounds(2), lambda: rounds(-(-SLOTS // cap))]
     )
-    return call(finish_kernel, shape(1, TP * WIDE), [VMEM])(over_plane(mixed))
+    return call(finish_kernel, shape(1, TP * WIDE), [VMEM])(over_far(mixed))
 
 
 def solution(mesh):
-    fine = Mesh(mesh.devices.reshape(-1, NY, TP // 2, 2), ("z", "y", "x", "c"))
-    own = ("z", "y", "x", "c")
+    fine = Mesh(
+        mesh.devices.reshape(FAR, -1, NY, TP // 2, 2), ("zh", "zl", "y", "x", "c")
+    )
+    own = fine.axis_names
     return jax.shard_map(
         functools.partial(per_device, 7),
         mesh=fine,
         in_specs=(
             P(own, None),
-            P(None, ("z", "y"), None, ("x", "c")),
-            P(("z", "y"), None),
-            P(("z", "y")),
+            P(None, own[:3], None, own[3:]),
+            P(own[:3], None),
+            P(own[:3]),
         ),
         out_specs=P(own, None),
         check_vma=False,

time: 89.6 us -> 76.1 us (0.85)
  blocking collectives: 84.8 us -> 70.8 us
    all_to_all x4, blocking collectives: 84.8 us -> 70.8 us  [the longest x2 48.8 us: over_far(): lax.all_to_all(x, ('zh', 'x', 'c'), 0, 0, tiled=True, axis_index_groups=t...]
where the time goes in v7:
time: 76.1 us; the launch traced here: 75.3 us
  blocking collectives  70.8 us (93%)
  Pallas kernels  4.4 us (6%)
    all_to_all x2, blocking collectives, over_far(): lax.all_to_all(x, ('zh', 'x', 'c'), 0, 0, tiled=True, axis_index_groups=t...  48.8 us
    all_to_all x2, blocking collectives, over_near(): x = lax.all_to_all(x, near, 0, 0, tiled=True, axis_index_groups=groups)  22 us

profile of v7, /device:TPU:1, one launch (start us, length us, event | category | flops | bytes accessed | tf_op | source)
XLA Modules:
  0.0 75.3 jit_solution(7102512672039542527)
XLA Ops:
  0.0 0.9 %shard_map.46 = bf16[32,2,640]{2,1,0:T(2,128)(2,1)S(1)} custom-call(bf16[1,8192]{1,0:T(2,128)(2,1)} %q_hbm.1, s32[4,8]{1,0:T(4,128)} %bitcast.43, s32[8]{0:T(128)} %len_hbm.1), custom_call_target="tpu_custom_call" | custom-call | tf_op jit(solution)/shard_map/pallas_call | solution.py:341
  0.9 26.1 %all_to_all.61.a_ref = bf16[32,2,640]{2,1,0:T(2,128)(2,1)S(1)} all-to-all(bf16[32,2,640]{2,1,0:T(2,128)(2,1)S(1)} %shard_map.46), channel_id=1, replica_groups={{260,261,262,263,256,257,258,259,388,389,390,391,384,385,386,387,4,5,6,..., dimensions={0} | all-to-all | bytes 163840 | tf_op jit(solution)/shard_map/all_to_all | solution.py:291
  27.0 0.0 copy-start
  27.0 0.5 shard_map.47
  27.5 11.1 %all_to_all.62 = bf16[16,8,1024]{2,1,0:T(8,128)(2,1)S(1)} all-to-all(bf16[16,8,1024]{2,1,0:T(8,128)(2,1)S(1)} %bitcast.37), channel_id=1, replica_groups={{80,88,64,72,112,120,96,104,16,24,0,8,48,56,32,40},{81,89,65,73,113,121..., dimensions={0} | all-to-all | bytes 524288 | tf_op jit(solution)/shard_map/all_to_all | solution.py:298
  38.6 0.0 copy-done
  38.6 1.5 %shard_map.48 = (bf16[128,1024]{1,0:T(8,128)(2,1)S(1)}, s32[1]{0:T(128)S(4)}) custom-call(bf16[128,1024]{1,0:T(8,128)(2,1)S(1)} %bitcast.34, bf16[2,32,256,128]{3,2,1,0:T(8,128)(2,1)S(1)} %copy-done), custom_call_target="tpu_custom_call" | custom-call | tf_op jit(solution)/shard_map/pallas_call | solution.py:311
  40.0 10.9 %all_to_all.63 = bf16[16,8,1024]{2,1,0:T(8,128)(2,1)S(1)} all-to-all(bf16[16,8,1024]{2,1,0:T(8,128)(2,1)S(1)} %bitcast.36), channel_id=1, replica_groups={{80,88,64,72,112,120,96,104,16,24,0,8,48,56,32,40},{81,89,65,73,113,121..., dimensions={0} | all-to-all | bytes 524288 | tf_op jit(solution)/shard_map/all_to_all | solution.py:298
  51.0 0.7 shard_map.49
  51.7 22.8 %all_to_all.64.d_ref = bf16[32,2,640]{2,1,0:T(2,128)(2,1)S(1)} all-to-all(bf16[32,2,640]{2,1,0:T(2,128)(2,1)S(1)} %get-tuple-element.75), channel_id=1, replica_groups={{260,261,262,263,256,257,258,259,388,389,390,391,384,385,386,387,4,5,6,..., dimensions={0} | all-to-all | bytes 163840 | tf_op jit(solution)/shard_map/all_to_all | solution.py:291
  74.5 0.8 %shard_map.50 = bf16[1,8192]{1,0:T(2,128)(2,1)} custom-call(bf16[32,2,640]{2,1,0:T(2,128)(2,1)S(1)} %all_to_all.64.d_ref), custom_call_target="tpu_custom_call" | custom-call | tf_op jit(solution)/shard_map/pallas_call | solution.py:363
  (1 shorter events, 0.0 us)
Async XLA Ops:
  27.0 11.6 %copy-start = (bf16[2,32,256,128]{3,2,1,0:T(8,128)(2,1)S(1)}, bf16[2,32,256,128]{3,2,1,0:T(8,128)(2,1)}, u32[]{:S(2)}) copy-start(bf16[2,32,256,128]{3,2,1,0:T(8,128)(2,1)} %kv_ref) | copy-start | bytes 12582916

commit v8 on v7

--- a/solution.py
+++ b/solution.py
@@ -70,7 +70,8 @@
     extra = jnp.where(lane == 9, (length % SLOTS).astype(F32), extra)
     q = q_ref[...].astype(F32)
     halves = [q[:, i * HALF : (i + 1) * HALF] for i in range(2 * TP)]
-    heads = jnp.concatenate(halves[TP:] + halves[:TP], axis=0)
+    order = [(p + TP // 2) % TP ^ 1 for p in range(TP)]
+    heads = jnp.concatenate([halves[2 * p + half] for p in order for half in range(2)], axis=0)
     both = jnp.concatenate([heads, extra], axis=1).reshape(TP, 2, LONG).astype(BF16)
     for far in range(FAR):
         out_ref[far * TP : (far + 1) * TP] = both
@@ -83,10 +84,14 @@
     both = a_ref[...].astype(F32).reshape(ROWS * 2, LONG)
     for k in range(SPAN + 1):
         scr[k] = both[:, k * HD : (k + 1) * HD]
+    def take(k, half):
+        parts = [scr[k, pl.ds(2 * c + half, ROWS // 2, stride=4), :] for c in range(2)]
+        return jnp.concatenate(parts, axis=0)
+
     query = jnp.concatenate(
-        [scr[k, pl.ds(half, ROWS, stride=2), :] for half in range(2) for k in range(SPAN)], axis=1
+        [take(k, half) for half in range(2) for k in range(SPAN)], axis=1
     ).astype(BF16)
-    extra = scr[SPAN, pl.ds(0, ROWS, stride=2), :].T
+    extra = take(SPAN, 0).T
     pool = jnp.concatenate([extra[b : b + 1] for b in range(MAXB)], axis=1)
     slot = jnp.concatenate([extra[MAXB + b : MAXB + b + 1] for b in range(MAXB)], axis=1)
     length = extra[8:9] * SLOTS + extra[9:10]
@@ -224,13 +229,18 @@
     extra = jnp.zeros((ROWS, HD), F32)
     for k, part in enumerate(three):
         extra = jnp.where(lane // GROUP == k, part, extra)
+
+    def put(k, half, x):
+        for c in range(2):
+            rows = pl.ds(2 * (1 - c) + half, ROWS // 2, stride=4)
+            scr[k, rows, :] = x[c * ROWS // 2 : (c + 1) * ROWS // 2]
+
     for half in range(2):
-        rows = pl.ds(half, ROWS, stride=2)
         for k in range(SPAN):
             g = half * SPAN + k
             mixed = [factor[b][:, g : g + 1] * got[b][:, g * HD : (g + 1) * HD] for b in range(MAXB)]
-            scr[k, rows, :] = functools.reduce(jnp.add, mixed)
-        scr[SPAN, rows, :] = extra
+            put(k, half, functools.reduce(jnp.add, mixed))
+        put(SPAN, half, extra)
     both = jnp.concatenate([scr[k] for k in range(SPAN + 1)], axis=1)
     out_ref[...] = both.reshape(ROWS, 2, LONG).astype(BF16)
 
@@ -287,9 +297,10 @@
     def turned(slow, fast):
         return [[(i + slow // 2) % slow * fast + (j + fast // 2) % fast for i in range(slow) for j in range(fast)]]
 
-    def over_far(x):
+    def over_far(x, core):
+        groups = [[place ^ core for place in turned(FAR, TP)[0]]]
         return lax.all_to_all(
-            x, ("zh", "x", "c"), 0, 0, tiled=True, axis_index_groups=turned(FAR, TP)
+            x, ("zh", "x", "c"), 0, 0, tiled=True, axis_index_groups=groups
         )
 
     def over_near(x):
@@ -349,7 +360,7 @@
             pltpu.SemaphoreType.DMA((3,)),
         ],
     )(*(pltpu.with_memory_space_constraint(x, pltpu.HBM) for x in (queries, block_table.T, lengths)))
-    rows = over_far(fanned)
+    rows = over_far(fanned, 1)
     out, place = pack(rows, 0)
     got = over_near(out)
     got, place, rows, kv_pool = lax.optimization_barrier((got, place, rows, kv_pool))
@@ -360,7 +371,7 @@
     mixed = lax.switch(
         over[0], [lambda: mixed, lambda: rounds(2), lambda: rounds(-(-SLOTS // cap))]
     )
-    return call(finish_kernel, shape(1, TP * WIDE), [VMEM])(over_far(mixed))
+    return call(finish_kernel, shape(1, TP * WIDE), [VMEM])(over_far(mixed, 0))
 
 
 def solution(mesh):

time: 76.1 us -> 77.3 us (1.016)
  blocking collectives: 70.8 us -> 72.2 us
    all_to_all x2, blocking collectives: 48.8 us -> 49.9 us  [over_far(): lax.all_to_all(x, ('zh', 'x', 'c'), 0, 0, tiled=True, axis_index_groups=g...]
where the time goes in v8:
time: 77.3 us; the launch traced here: 76.7 us
  blocking collectives  72.2 us (93%)
  Pallas kernels  4.42 us (6%)
    all_to_all x2, blocking collectives, over_far(): lax.all_to_all(x, ('zh', 'x', 'c'), 0, 0, tiled=True, axis_index_groups=g...  49.9 us
    all_to_all x2, blocking collectives, over_near(): x = lax.all_to_all(x, near, 0, 0, tiled=True, axis_index_groups=groups)  22.3 us

profile of v8, /device:TPU:1, one launch (start us, length us, event | category | flops | bytes accessed | tf_op | source)
XLA Modules:
  0.0 76.7 jit_solution(11052447954792719691)
XLA Ops:
  0.0 0.9 %shard_map.46 = bf16[32,2,640]{2,1,0:T(2,128)(2,1)S(1)} custom-call(bf16[1,8192]{1,0:T(2,128)(2,1)} %q_hbm.1, s32[4,8]{1,0:T(4,128)} %bitcast.43, s32[8]{0:T(128)} %len_hbm.1), custom_call_target="tpu_custom_call" | custom-call | tf_op jit(solution)/shard_map/pallas_call | solution.py:352
  0.9 25.9 %all_to_all.61.a_ref = bf16[32,2,640]{2,1,0:T(2,128)(2,1)S(1)} all-to-all(bf16[32,2,640]{2,1,0:T(2,128)(2,1)S(1)} %shard_map.46), channel_id=1, replica_groups={{261,260,263,262,257,256,259,258,389,388,391,390,385,384,387,386,5,4,7,..., dimensions={0} | all-to-all | bytes 163840 | tf_op jit(solution)/shard_map/all_to_all | solution.py:302
  26.8 0.0 copy-start
  26.8 0.5 shard_map.47
  27.3 11.5 %all_to_all.62 = bf16[16,8,1024]{2,1,0:T(8,128)(2,1)S(1)} all-to-all(bf16[16,8,1024]{2,1,0:T(8,128)(2,1)S(1)} %bitcast.37), channel_id=1, replica_groups={{80,88,64,72,112,120,96,104,16,24,0,8,48,56,32,40},{81,89,65,73,113,121..., dimensions={0} | all-to-all | bytes 524288 | tf_op jit(solution)/shard_map/all_to_all | solution.py:309
  38.9 0.0 copy-done
  38.9 1.5 %shard_map.48 = (bf16[128,1024]{1,0:T(8,128)(2,1)S(1)}, s32[1]{0:T(128)S(4)}) custom-call(bf16[128,1024]{1,0:T(8,128)(2,1)S(1)} %bitcast.34, bf16[2,32,256,128]{3,2,1,0:T(8,128)(2,1)S(1)} %copy-done), custom_call_target="tpu_custom_call" | custom-call | tf_op jit(solution)/shard_map/pallas_call | solution.py:322
  40.4 10.8 %all_to_all.63 = bf16[16,8,1024]{2,1,0:T(8,128)(2,1)S(1)} all-to-all(bf16[16,8,1024]{2,1,0:T(8,128)(2,1)S(1)} %bitcast.36), channel_id=1, replica_groups={{80,88,64,72,112,120,96,104,16,24,0,8,48,56,32,40},{81,89,65,73,113,121..., dimensions={0} | all-to-all | bytes 524288 | tf_op jit(solution)/shard_map/all_to_all | solution.py:309
  51.1 0.7 shard_map.49
  51.9 24.0 %all_to_all.64.d_ref = bf16[32,2,640]{2,1,0:T(2,128)(2,1)S(1)} all-to-all(bf16[32,2,640]{2,1,0:T(2,128)(2,1)S(1)} %get-tuple-element.75), channel_id=1, replica_groups={{260,261,262,263,256,257,258,259,388,389,390,391,384,385,386,387,4,5,6,..., dimensions={0} | all-to-all | bytes 163840 | tf_op jit(solution)/shard_map/all_to_all | solution.py:302
  75.9 0.8 %shard_map.50 = bf16[1,8192]{1,0:T(2,128)(2,1)} custom-call(bf16[32,2,640]{2,1,0:T(2,128)(2,1)S(1)} %all_to_all.64.d_ref), custom_call_target="tpu_custom_call" | custom-call | tf_op jit(solution)/shard_map/pallas_call | solution.py:374
  (1 shorter events, 0.0 us)
Async XLA Ops:
  26.8 12.1 %copy-start = (bf16[2,32,256,128]{3,2,1,0:T(8,128)(2,1)S(1)}, bf16[2,32,256,128]{3,2,1,0:T(8,128)(2,1)}, u32[]{:S(2)}) copy-start(bf16[2,32,256,128]{3,2,1,0:T(8,128)(2,1)} %kv_ref) | copy-start | bytes 12582916
